TPU v7x, 512 devices: a whole 4x8x8 slice. The times are simulated.
512 devices in a mesh: freq: 128 (over z, y, core), pol: 4 (over x).
Axes of the slice: x: 4, y: 8, z: 8, core: 2. Of those that a mesh axis runs over, the one named last changes fastest.
Arguments:
- voltages: bfloat16 [128, 4, 1392, 2, 512], P('freq', 'pol'), as said below
- gains: float32 [128, 4, 2, 512], P('freq', 'pol'), as said below
- slopes: int32 [2048], replicated, may hold values from 0 to 48, as said below
- mask: int32 [2048], replicated, may hold values from 0 to 1, as said below
Outputs:
- dedispersed: float32 [1024, 24, 96], P('freq', None, 'pol')
Inputs may be any that keep to these rules, and one draw needn't show every extreme that they name: `voltages`: real and imaginary parts of each feed's voltage in each coarse channel, group and sample. `gains`: complex gain of each feed in each coarse channel and group. `slopes`: some fine channel has the slope 48. `mask`: 1 marks a live fine channel; the middle fine channel is live.
All inputs are finite; a program needn't handle non-finite values.
Results may differ from a plain program's by a relative error of at most 0.025.
The roundings to bfloat16 on the way count: a program that leaves them out, or rounds other values in their place, can miss the bound.
Values may be sent and summed in bfloat16 or wider, within the bound.
No kernel may reach another device: no remote copies, remote signals or barrier semaphores. Data moves between devices by JAX's collectives and lax.ppermute only.
A program may use at most 64 MiB of HBM per device.

v0:
```python
import math

import jax
import jax.numpy as jnp
from jax import lax
from jax.sharding import PartitionSpec as P

BEAMS = 1024
UP = 16
TAPS = 16
DM = 96
MAXD = 48
TOUT = 24
FR = 72


EPSILON = 1e-06
HIGHEST = lax.Precision.HIGHEST


def beam_table(feed_count, beam_order):
    feed_index = jnp.arange(feed_count, dtype=jnp.int32)[:, None]
    turn_count = feed_index * beam_order[None, :] % BEAMS
    angles = turn_count.astype(jnp.float32) * (2.0 * math.pi / BEAMS)
    norm_scale = 1.0 / math.sqrt(feed_count)
    cosine = jnp.cos(angles) * norm_scale
    sine_table = jnp.sin(angles) * norm_scale
    top_rows = jnp.concatenate([cosine, -sine_table], axis=1)
    bottom_rows = jnp.concatenate([sine_table, cosine], axis=1)
    return jnp.concatenate([top_rows, bottom_rows], axis=0).astype(jnp.bfloat16)


def filter_taps():
    length = TAPS * UP
    position = jnp.arange(length, dtype=jnp.float32) + 0.5
    hann_window = 0.5 - 0.5 * jnp.cos(2.0 * math.pi * position / length)
    values = jnp.sinc((position - 0.5 * length) / UP) * hann_window
    return values.reshape(TAPS, UP).astype(jnp.bfloat16)


def band_matrix(block_count):
    coeffs = filter_taps().astype(jnp.float32)
    time_lag = (
        jnp.arange(block_count, dtype=jnp.int32)[None, :] - jnp.arange(FR, dtype=jnp.int32)[:, None]
    )
    select = (time_lag[None, :, :] == jnp.arange(TAPS, dtype=jnp.int32)[:, None, None]).astype(
        jnp.float32
    )
    return jnp.einsum("pn,pmq->nmq", coeffs, select, precision=HIGHEST).astype(jnp.bfloat16)


def fourier_tables():
    freq_index = jnp.arange(UP, dtype=jnp.int32)
    turn_count = freq_index[:, None] * freq_index[None, :] % UP
    angles = turn_count.astype(jnp.float32) * (2.0 * math.pi / UP)
    return (jnp.cos(angles), jnp.sin(angles))


def calibrate(voltage, gain_group):
    real_v = voltage[:, :, 0, :].astype(jnp.float32)
    imag_v = voltage[:, :, 1, :].astype(jnp.float32)
    real_g = gain_group[:, None, 0, :]
    imag_g = gain_group[:, None, 1, :]
    real_x = real_v * real_g - imag_v * imag_g
    imag_x = real_v * imag_g + imag_v * real_g
    return jnp.concatenate([real_x, imag_x], axis=-1).astype(jnp.bfloat16)


def fine_power(formed):
    channel_count = formed.shape[0]
    block_count = formed.shape[1] // UP
    blocks = formed.reshape(channel_count, block_count, UP, 2 * BEAMS)
    windowed = jnp.einsum(
        "cqnb,nmq->cmnb", blocks, band_matrix(block_count), preferred_element_type=jnp.float32
    )
    cosine, sine_table = fourier_tables()
    real_in = windowed[..., :BEAMS]
    imag_in = windowed[..., BEAMS:]
    real_out = jnp.einsum("cmnb,kn->bckm", real_in, cosine, precision=HIGHEST) + jnp.einsum(
        "cmnb,kn->bckm", imag_in, sine_table, precision=HIGHEST
    )
    imag_out = jnp.einsum("cmnb,kn->bckm", imag_in, cosine, precision=HIGHEST) - jnp.einsum(
        "cmnb,kn->bckm", real_in, sine_table, precision=HIGHEST
    )
    return real_out * real_out + imag_out * imag_out


def channel_totals(summed, ch_dev):
    return jnp.sum(summed.astype(jnp.float32).reshape(-1, ch_dev, UP, FR), axis=(0, 3))


def normalize(summed, totals, live_mask, ch_dev):
    channel_mean = totals / (BEAMS * FR)
    shaped = summed.reshape(summed.shape[:3] + (ch_dev, UP, FR)).astype(jnp.float32)
    relative = shaped / (channel_mean[:, :, None] + EPSILON)
    normed = (live_mask * (relative - 1.0)).astype(jnp.bfloat16)
    return normed.reshape(summed.shape)


def dedisperse(normed, slopes, trials, live_total):
    delays = trials[None, :] * slopes[:, None] // (DM - 1)
    initial = jnp.zeros((normed.shape[0], TOUT, trials.shape[0]), jnp.float32)

    def add_delay(delay_step, total_sum):
        window = lax.dynamic_slice_in_dim(normed, delay_step, TOUT, 2)
        picked = (delays == delay_step).astype(jnp.bfloat16)
        return total_sum + jnp.einsum(
            "bct,cd->btd", window, picked, preferred_element_type=jnp.float32
        )

    return lax.fori_loop(0, MAXD + 1, add_delay, initial) / jnp.sqrt(live_total)


def on_device(voltages, gains, slopes, mask):
    freq_count = lax.axis_size("freq")
    pol_count = lax.axis_size("pol")
    ch_dev = voltages.shape[0]
    time_count = voltages.shape[2]
    feed_count = voltages.shape[4]
    per_block = BEAMS // (freq_count * pol_count)
    trial_share = DM // pol_count
    column = jnp.arange(BEAMS, dtype=jnp.int32)
    owner_group = column // (freq_count * per_block)
    owner_freq = column // per_block % freq_count
    beam_order = owner_freq * (pol_count * per_block) + owner_group * per_block + column % per_block
    weights = beam_table(feed_count, beam_order)
    calibrated = calibrate(voltages[:, 0], gains[:, 0])
    formed = jnp.dot(
        calibrated.reshape(ch_dev * time_count, 2 * feed_count),
        weights,
        preferred_element_type=jnp.float32,
    )
    formed = formed.astype(jnp.bfloat16).reshape(ch_dev, time_count, 2 * BEAMS)
    beam_power = fine_power(formed).astype(jnp.bfloat16)
    power_terms = beam_power.astype(jnp.float32).reshape(
        pol_count, freq_count, per_block, ch_dev, UP * FR
    )
    own_start = lax.axis_index("freq") * (ch_dev * UP)
    live_mask = (
        lax.dynamic_slice_in_dim(mask, own_start, ch_dev * UP)
        .astype(jnp.float32)
        .reshape(ch_dev, UP, 1)
    )
    live_total = jnp.sum(mask).astype(jnp.float32)
    quarter_trials = lax.axis_index("pol") * trial_share + jnp.arange(trial_share, dtype=jnp.int32)
    summed = lax.psum(power_terms.astype(jnp.bfloat16), "pol")
    totals = channel_totals(summed, ch_dev)
    normed = normalize(summed, totals, live_mask, ch_dev)
    turned = lax.all_to_all(normed, "freq", split_axis=1, concat_axis=3, tiled=True)
    dedispersed = dedisperse(
        turned.reshape(pol_count * per_block, -1, FR), slopes, quarter_trials, live_total
    )
    return dedispersed


def solution(mesh):
    placed = (P("freq", "pol", None, None, None), P("freq", "pol", None, None), P(), P())
    return jax.shard_map(
        on_device, mesh=mesh, in_specs=placed, out_specs=P("freq", None, "pol"), check_vma=False
    )
```

profile of v0, /device:TPU:1, one launch (start us, length us, event | category | flops | bytes accessed | tf_op | source)
XLA Modules:
  0.0 313.3 jit_solution(17321962522803680671)
XLA Ops:
  6.6 7.3 %fusion.155 = (bf16[1,1392,1,512]{3,2,1,0:T(2,128)(2,1)S(1)}, f32[1,1392,1,512]{3,2,1,0:T(1,128)S(1)}) fusion(bf16[1,1392,2,512]{3,2,1,0:T(2,128)(2,1)} %bitcast.63), kind=kLoop, calls=%fused_computation.199 | loop fusion | flops 712704 | bytes 7127040 | tf_op jit(solution)/shard_map/slice | solution.py:60
  13.9 8.8 %negate_convert_fusion = (bf16[512,1024]{1,0:T(8,128)(2,1)S(1)}, bf16[512,1024]{1,0:T(8,128)(2,1)S(1)}, bf16[512,1024]{1,0:T(8,128)(2,1)S(1)}) fusion(s32[1024]{0:T(1024)S(1)} %fusion.97), kind=kLoop, calls=%fused_computation.70 | loop fusion | flops 10485760 | bytes 3149824 | tf_op jit(solution)/shard_map/convert.8
  23.0 0.9 fusion.44
  23.9 19.9 %convolution_convert_fusion = bf16[1392,2048]{1,0:T(8,128)(2,1)S(1)} fusion(bf16[512,1024]{1,0:T(8,128)(2,1)S(1)} %get-tuple-element.147, bf16[512,1024]{1,0:T(8,128)(2,1)S(1)} %get-tuple-element.146, bf16[512,1024]{1,0:T(8,128)(2,1)S(1)} %get-tuple-element.145, bf16[1392,512]{1,0:T(8,128)(2,1)S(1)} %get-tuple-element.140, ...), kind=kOutput, calls=%fused_computation.23 | convolution fusion | flops 5863800832 | bytes 11698176 | tf_op jit(solution)/shard_map/dot_general | solution.py:128
  43.8 7.4 %fusion.25 = f32[1,72,16,2048]{3,1,2,0:T(8,128)S(1)} fusion(bf16[87,16,2048]{2,1,0:T(8,128)(2,1)S(1)} %bitcast.62, bf16[16,72,87]{2,0,1:T(8,128)(2,1)S(1)} %convolution_convert_fusion.1), kind=kOutput, calls=%fused_computation.34 | convolution fusion | flops 410517504 | bytes 15339264 | tf_op jit(solution)/shard_map/cqnb,nmq->cmnb/dot_general | solution.py:73
  51.2 1.9 slice_bitcast_fusion.1
  53.1 6.7 %fusion.28 = f32[16,72,1024]{2,0,1:T(8,128)S(1)} fusion(f32[72,16,1024]{2,0,1:T(8,128)S(1)} %get-tuple-element.138), kind=kOutput, calls=%fused_computation.35 | convolution fusion | flops 226496000 | bytes 9437184 | tf_op jit(solution)/shard_map/cmnb,kn->bckm/dot_general | solution.py:82
  59.8 6.7 %fusion.30 = f32[16,72,1024]{2,0,1:T(8,128)S(1)} fusion(f32[72,16,1024]{2,0,1:T(8,128)S(1)} %get-tuple-element.138), kind=kOutput, calls=%fused_computation.37 | convolution fusion | flops 226496000 | bytes 9437184 | tf_op jit(solution)/shard_map/cmnb,kn->bckm/dot_general | solution.py:79
  66.5 6.8 %fusion.32 = f32[16,72,1024]{2,0,1:T(8,128)S(1)} fusion(f32[72,16,1024]{2,0,1:T(8,128)S(1)} %get-tuple-element.137), kind=kOutput, calls=%fused_computation.39 | convolution fusion | flops 226496000 | bytes 9437184 | tf_op jit(solution)/shard_map/cmnb,kn->bckm/dot_general | solution.py:82
  73.3 7.0 %fusion.50 = bf16[1024,1,16,72]{0,2,3,1:T(8,128)(2,1)S(1)} fusion(f32[16,72,1024]{2,0,1:T(8,128)S(1)} %fusion.28, f32[16,72,1024]{2,0,1:T(8,128)S(1)} %fusion.32, f32[16,72,1024]{2,0,1:T(8,128)S(1)} %fusion.30, f32[72,16,1024]{2,0,1:T(8,128)S(1)} %get-tuple-element.137), kind=kOutput, calls=%fused_computation.65 | convolution fusion | flops 233573888 | bytes 21233664 | tf_op jit(solution)/shard_map/cmnb,kn->bckm/dot_general | solution.py:79
  80.3 5.2 %copy.49 = bf16[1024,1,16,72]{3,2,0,1:T(8,128)(2,1)} copy(bf16[1024,1,16,72]{0,2,3,1:T(8,128)(2,1)S(1)} %fusion.50) | data formatting | bytes 4718592 | tf_op jit(solution)/shard_map/convert_element_type | solution.py:134
  85.5 10.0 %convert_element_type.111 = bf16[4,128,2,1,1152]{4,2,1,0,3:T(2,128)(2,1)S(1)} reshape(bf16[1024,1,16,72]{3,2,0,1:T(8,128)(2,1)} %copy.49) | data formatting | bytes 4718592 | tf_op jit(solution)/shard_map/convert_element_type | solution.py:146
  95.5 1.8 copy.50
  97.6 79.1 %all-reduce.2.cloned.1.call-done = bf16[4,128,2,1,1152]{4,1,3,2,0:T(8,128)(2,1)} async-done(((bf16[4,128,2,1,1152]{4,1,3,2,0:T(8,128)(2,1)}), bf16[4,128,2,1,1152]{4,1,3,2,0:T(8,128)(2,1)}) %all-reduce.2.cloned.1.call-update) | async-done | bytes 2359312 | tf_op jit(solution)/shard_map/psum | solution.py:146
  176.7 2.1 convert_reduce_fusion
  179.1 2.4 fusion.24
  181.5 3.8 %copy.51 = bf16[4,128,2,1,1152]{4,2,0,3,1:T(2,128)(2,1)} copy(bf16[4,128,2,1,1152]{4,1,3,2,0:T(8,128)(2,1)S(1)} %fusion.24) | data formatting | bytes 4718592 | tf_op jit(solution)/shard_map/convert_element_type | solution.py:96
  185.3 14.7 %all-to-all-start = ((bf16[4,128,2,1,1152]{4,2,0,3,1:T(2,128)(2,1)}), bf16[4,128,2,1,1152]{4,2,0,3,1:T(2,128)(2,1)}, u32[]{:S(2)}, u32[]{:S(2)}) async-start(bf16[4,128,2,1,1152]{4,2,0,3,1:T(2,128)(2,1)} %copy.51), calls=%async_computation | async-start | bytes 4718592 | tf_op jit(solution)/shard_map/all_to_all | solution.py:149
  201.3 55.2 %all-to-all-done = bf16[4,128,2,1,1152]{4,2,0,3,1:T(2,128)(2,1)} async-done(((bf16[4,128,2,1,1152]{4,2,0,3,1:T(2,128)(2,1)}), bf16[4,128,2,1,1152]{4,2,0,3,1:T(2,128)(2,1)}, u32[]{:S(2)}, u32[]{:S(2)}) %all-to-all-start) | async-done | bytes 2359328 | tf_op jit(solution)/shard_map/all_to_all | solution.py:149
  256.5 2.0 copy.80
  258.5 8.3 %reshape.216 = bf16[8,2048,72]{2,1,0:T(8,128)(2,1)} reshape(bf16[4,1,2,128,1,1152]{5,3,4,2,1,0:T(8,128)(2,1)S(1)} %bitcast.64) | data formatting | bytes 4718592 | tf_op jit(solution)/shard_map/reshape | solution.py:151
  266.9 4.8 %copy.53 = bf16[8,2048,72]{1,2,0:T(8,128)(2,1)S(1)} copy(bf16[8,2048,72]{2,1,0:T(8,128)(2,1)} %reshape.216) | data formatting | bytes 4718592
  271.7 33.8 %while.14 = (s32[]{:T(128)}, f32[8,24,24]{2,1,0:T(8,128)S(1)}, bf16[8,2048,72]{1,2,0:T(8,128)(2,1)S(1)}, s32[2048]{0:T(1024)S(1)}, s32[24]{0:T(128)S(1)}, /*index=5*/s32[]{:T(128)}, s32[]{:T(128)}) while((s32[]{:T(128)}, f32[8,24,24]{2,1,0:T(8,128)S(1)}, bf16[8,2048,72]{1,2,0:T(8,128)(2,1)S(1)}, s32[2048]{0:T(1024)S(1)}, ...), condition=%wide.region_4.5_spmd.clone, body=%wide.region_3.4_spmd.clone.sunk | while | flops 19375108 | bytes 912983 | solution.py:111
  271.7 0.7 convolution_add_fusion.2
  272.4 0.7 convolution_add_fusion.2
  273.1 0.7 convolution_add_fusion.2
  273.8 0.7 convolution_add_fusion.2
  274.5 0.7 convolution_add_fusion.2
  275.2 0.7 convolution_add_fusion.2
  275.9 0.7 convolution_add_fusion.2
  276.5 0.7 convolution_add_fusion.2
  277.2 0.7 convolution_add_fusion.2
  277.9 0.7 convolution_add_fusion.2
  278.6 0.7 convolution_add_fusion.2
  279.3 0.7 convolution_add_fusion.2
  280.0 0.7 convolution_add_fusion.2
  280.7 0.7 convolution_add_fusion.2
  281.4 0.7 convolution_add_fusion.2
  282.1 0.7 convolution_add_fusion.2
  282.8 0.7 convolution_add_fusion.2
  283.5 0.7 convolution_add_fusion.2
  284.1 0.7 convolution_add_fusion.2
  284.8 0.7 convolution_add_fusion.2
  285.5 0.7 convolution_add_fusion.2
  286.2 0.7 convolution_add_fusion.2
  286.9 0.7 convolution_add_fusion.2
  287.6 0.7 convolution_add_fusion.2
  288.3 0.7 convolution_add_fusion.2
  289.7 0.7 convolution_add_fusion.2
  290.4 0.7 convolution_add_fusion.2
  291.7 0.7 convolution_add_fusion.2
  292.4 0.7 convolution_add_fusion.2
  293.8 0.7 convolution_add_fusion.2
  294.5 0.7 convolution_add_fusion.2
  295.9 0.7 convolution_add_fusion.2
  296.6 0.7 convolution_add_fusion.2
  298.0 0.7 convolution_add_fusion.2
  298.6 0.7 convolution_add_fusion.2
  300.0 0.7 convolution_add_fusion.2
  300.7 0.7 convolution_add_fusion.2
  301.4 0.7 convolution_add_fusion.2
  302.8 0.7 convolution_add_fusion.2
  303.5 0.7 convolution_add_fusion.2
  304.9 0.7 convolution_add_fusion.2
  (32 shorter events, 7.6 us)
Async XLA Ops:
  6.5 170.1 %all-reduce.2.cloned.1.call-start = ((), (), s32[]{:S(2)}) async-start(), calls=%async_computation.1 | async-start | bytes 4718592 | tf_op jit(solution)/shard_map/psum | solution.py:146
  6.6 7.3 %copy-start.1 = (f32[1,1,2,512]{3,2,1,0:T(2,128)S(1)}, f32[1,1,2,512]{3,2,1,0:T(2,128)}, u32[]{:S(2)}) copy-start(f32[1,1,2,512]{3,2,1,0:T(2,128)} %param.7) | copy-start | bytes 12292
  95.5 1.8 copy-start
  185.3 71.2 %all-to-all-start = ((bf16[4,128,2,1,1152]{4,2,0,3,1:T(2,128)(2,1)}), bf16[4,128,2,1,1152]{4,2,0,3,1:T(2,128)(2,1)}, u32[]{:S(2)}, u32[]{:S(2)}) async-start(bf16[4,128,2,1,1152]{4,2,0,3,1:T(2,128)(2,1)} %copy.51), calls=%async_computation | async-start | bytes 4718592 | tf_op jit(solution)/shard_map/all_to_all | solution.py:149
  266.9 4.8 %copy-start.2 = (s32[2048]{0:T(1024)S(1)}, s32[2048]{0:T(1024)}, u32[]{:S(2)}) copy-start(s32[2048]{0:T(1024)} %param.8) | copy-start | bytes 24580
Sparse Core Ops, SparseCore 0:
  97.5 79.1 all-reduce.1
where the time goes:
time: 319 us; the launch traced here: 313 us
  waiting for transfers between devices  134 us (42%)
  matrix products  87.6 us (27%)
  local copies, waits for them, and re-layouts  38.3 us (12%)
  other arithmetic  23 us (7%)
  starting transfers between devices  14.7 us (5%)
  between operations  14.4 us (5%)
    psum x1, waiting for transfers between devices, on_device(): summed = lax.psum(power_terms.astype(jnp.bfloat16), 'pol')  79.1 us
    all_to_all x1, waiting for transfers between devices, on_device(): lax.all_to_all(normed, 'freq', split_axis=1, concat_axis=3, tiled=True)  55.2 us
    dot_general x49, matrix products, add_delay(): jnp.einsum('bct,cd->btd', window, picked, preferred_element_type=jnp.floa...  32.8 us
    dot_general x1, matrix products, on_device(): jnp.dot(calibrated.reshape(ch_dev * time_count, 2 * feed_count), weights,...  19.9 us
    all_to_all x1, starting transfers between devices, on_device(): lax.all_to_all(normed, 'freq', split_axis=1, concat_axis=3, tiled=True)  14.7 us
    convert_element_type x2, local copies, waits for them, and re-layouts, on_device(): summed = lax.psum(power_terms.astype(jnp.bfloat16), 'pol')  11.8 us
    another operation x2, other arithmetic  9.75 us
    reshape x1, local copies, waits for them, and re-layouts, on_device(): turned.reshape(pol_count * per_block, -1, FR)  8.33 us
  transfers between devices with their start and end apart: 2, of which 2 were waited for; matrix products, arithmetic and copies ran while one was open for 0% of the time, Pallas kernels for 0%

commit v1 on v0

v1 whole, which is shorter than its diff:
```python
import functools
import math

import jax
import jax.numpy as jnp
import ml_dtypes
import numpy as np
from jax import lax
from jax.experimental import pallas as pl
from jax.experimental.pallas import tpu as pltpu
from jax.sharding import PartitionSpec as P

FEEDS = 512
BEAMS = 1024
UP = 16
TAPS = 16
DM = 96
MAXD = 48
TOUT = 24
FR = 72
TS = 1392
POL = 4
FREQ = 128
PAIR = BEAMS // (POL * FREQ)
QUARTER = FREQ * PAIR
MG = 8
BLOCKS = FR // MG
ROWS = UP * MG
SPAN = (MG - 1 + TAPS) * UP
SLOTS = 64
USED = 56
TILES = FEEDS // 128
EPSILON = 1e-06
BF16 = ml_dtypes.bfloat16
VMEM_LIMIT = 48 * 1024 * 1024


@functools.lru_cache(None)
def beam_tables():
    n = np.arange(FEEDS)[:, None]
    f = np.arange(FREQ)[:, None]
    b = np.arange(PAIR)[None, :]
    out = []
    for q in range(POL):
        k = (f * (POL * PAIR) + q * PAIR + b).reshape(1, -1)
        turn = (n * k) % BEAMS
        angle = turn.astype(np.float32) * np.float32(2.0 * math.pi / BEAMS)
        scale = np.float32(1.0 / math.sqrt(FEEDS))
        c = np.cos(angle) * scale
        s = np.sin(angle) * scale
        top = np.concatenate([c, -s], axis=1)
        low = np.concatenate([s, c], axis=1)
        out.append(np.concatenate([top, low], axis=0))
    return np.stack(out).astype(BF16)


@functools.lru_cache(None)
def bank_matrix():
    length = TAPS * UP
    pos = np.arange(length, dtype=np.float64) + 0.5
    hann = 0.5 - 0.5 * np.cos(2.0 * math.pi * pos / length)
    taps = (np.sinc((pos - 0.5 * length) / UP) * hann).astype(np.float32).astype(BF16)
    taps = taps.astype(np.float64)
    real = np.zeros((2, UP, MG, SPAN))
    imag = np.zeros((2, UP, MG, SPAN))
    lag = np.arange(length)
    for u in range(UP):
        angle = 2.0 * math.pi * ((u * lag) % UP) / UP
        c, s = taps * np.cos(angle), taps * np.sin(angle)
        for m in range(MG):
            at = slice(m * UP, m * UP + length)
            real[0, u, m, at], imag[0, u, m, at] = c, s
            real[1, u, m, at], imag[1, u, m, at] = -s, c
    both = np.concatenate([real.reshape(2 * ROWS, SPAN), imag.reshape(2 * ROWS, SPAN)], axis=1)
    return both.astype(np.float32).astype(BF16)


@functools.lru_cache(None)
def fold_matrix():
    g, u, m8 = np.meshgrid(np.arange(BLOCKS), np.arange(UP), np.arange(MG), indexing="ij")
    m = (g * MG + m8).reshape(-1)
    return (m[:, None] == np.arange(128)[None, :]).astype(np.float32).astype(BF16)


def first_slope(delay):
    return 8 * (delay // 8)


@functools.lru_cache(None)
def trial_matrix():
    parts = []
    share = DM // POL
    for delay in range(MAXD + 1):
        slope = np.arange(first_slope(delay), USED)
        block = np.zeros((POL * 32, slope.size), np.float32)
        for d in range(DM):
            block[(d // share) * 32 + d % share] = ((d * slope) // (DM - 1) == delay) & (slope <= MAXD)
        parts.append(block)
    full = np.concatenate(parts, axis=1)
    return full.astype(BF16)


STACK = sum(USED - first_slope(delay) for delay in range(MAXD + 1))


def calibrate_kernel(v_ref, g_ref, out_ref, wide):
    rows = out_ref.shape[0]
    wide[...] = v_ref[...].astype(jnp.float32)
    for j in range(TILES):
        lanes = slice(j * 128, (j + 1) * 128)
        re = wide[pl.ds(2 * j, rows, stride=2 * TILES), :]
        im = wide[pl.ds(2 * j + 1, rows, stride=2 * TILES), :]
        gr = g_ref[0:1, lanes]
        gi = g_ref[1:2, lanes]
        out_ref[:, lanes] = (re * gr - im * gi).astype(jnp.bfloat16)
        out_ref[:, FEEDS + j * 128 : FEEDS + (j + 1) * 128] = (re * gi + im * gr).astype(jnp.bfloat16)


def calibrate(voltages, gains):
    block = 464
    flat = voltages.reshape(TS, 2, TILES, 128).transpose(0, 2, 1, 3).reshape(TS * TILES * 2, 128)
    return pl.pallas_call(
        calibrate_kernel,
        grid=(TS // block,),
        in_specs=[
            pl.BlockSpec((block * 2 * TILES, 128), lambda i: (i, 0)),
            pl.BlockSpec((2, FEEDS), lambda i: (0, 0)),
        ],
        out_specs=pl.BlockSpec((block, 2 * FEEDS), lambda i: (i, 0)),
        out_shape=jax.ShapeDtypeStruct((TS, 2 * FEEDS), jnp.bfloat16),
        scratch_shapes=[pltpu.VMEM((block * 2 * TILES, 128), jnp.float32)],
        compiler_params=pltpu.CompilerParams(vmem_limit_bytes=VMEM_LIMIT),
        name="calibrate",
    )(flat, gains)


def power_kernel(q_ref, cal_ref, tab_ref, bank_ref, out_ref, tot_ref, formed):
    del q_ref
    for i in range(3):
        rows = slice(i * 464, (i + 1) * 464)
        formed[rows, :] = jnp.dot(
            cal_ref[rows, :], tab_ref[...], preferred_element_type=jnp.float32
        ).astype(jnp.bfloat16)
    total = jnp.zeros((ROWS, QUARTER), jnp.float32)
    for g in range(BLOCKS):
        rows = slice(g * ROWS, g * ROWS + SPAN)
        both = jnp.concatenate([formed[rows, :QUARTER], formed[rows, QUARTER:]], axis=0)
        fine = jnp.dot(bank_ref[...], both, preferred_element_type=jnp.float32)
        re, im = fine[:ROWS], fine[ROWS:]
        power = (re * re + im * im).astype(jnp.bfloat16)
        out_ref[g * ROWS : (g + 1) * ROWS, :] = power
        total = total + power.astype(jnp.float32)
    for u in range(UP):
        part = total[u * MG : (u + 1) * MG]
        tot_ref[u : u + 1, :] = jnp.broadcast_to(jnp.sum(part, keepdims=True), (1, 128))


def quarter_power(index, calibrated, tables, bank):
    return pl.pallas_call(
        power_kernel,
        grid_spec=pltpu.PrefetchScalarGridSpec(
            num_scalar_prefetch=1,
            grid=(1,),
            in_specs=[
                pl.BlockSpec((TS, 2 * FEEDS), lambda i, q: (0, 0)),
                pl.BlockSpec((None, 2 * FEEDS, 2 * QUARTER), lambda i, q: (q[0], 0, 0)),
                pl.BlockSpec((2 * ROWS, 2 * SPAN), lambda i, q: (0, 0)),
            ],
            out_specs=[
                pl.BlockSpec((UP * FR, QUARTER), lambda i, q: (0, 0)),
                pl.BlockSpec((UP, 128), lambda i, q: (0, 0)),
            ],
            scratch_shapes=[pltpu.VMEM((TS, 2 * QUARTER), jnp.bfloat16)],
        ),
        out_shape=[
            jax.ShapeDtypeStruct((UP * FR, QUARTER), jnp.bfloat16),
            jax.ShapeDtypeStruct((UP, 128), jnp.float32),
        ],
        compiler_params=pltpu.CompilerParams(vmem_limit_bytes=VMEM_LIMIT),
        cost_estimate=pl.CostEstimate(
            flops=2 * TS * 2 * FEEDS * 2 * QUARTER, bytes_accessed=5_000_000, transcendentals=0
        ),
        name="quarter_power",
    )(index.reshape(1), calibrated, tables, bank)


def normalize_kernel(tot_ref, a_ref, b_ref, c_ref, d_ref, out_ref, inverse):
    for u in range(UP):
        mean = tot_ref[u : u + 1, :] * (1.0 / (BEAMS * FR))
        inverse[u * MG : (u + 1) * MG, :] = jnp.broadcast_to(1.0 / (mean + EPSILON), (MG, 128))
    scale = jnp.concatenate([inverse[...]] * (QUARTER // 128), axis=1)
    for g in range(BLOCKS):
        rows = slice(g * ROWS, (g + 1) * ROWS)
        total = a_ref[rows, :].astype(jnp.float32) + b_ref[rows, :].astype(jnp.float32)
        total = total + c_ref[rows, :].astype(jnp.float32) + d_ref[rows, :].astype(jnp.float32)
        summed = total.astype(jnp.bfloat16).astype(jnp.float32)
        normed = summed * scale - 1.0
        out_ref[:, rows] = normed.T.astype(jnp.bfloat16)


def normalize(totals, parts):
    return pl.pallas_call(
        normalize_kernel,
        out_shape=jax.ShapeDtypeStruct((QUARTER, UP * FR), jnp.bfloat16),
        scratch_shapes=[pltpu.VMEM((ROWS, 128), jnp.float32)],
        compiler_params=pltpu.CompilerParams(vmem_limit_bytes=VMEM_LIMIT),
        name="normalize",
    )(totals, *parts)


def dedisperse_kernel(scale_ref, x_ref, hot_ref, fold_ref, trial_ref, out_ref, by_slope, stack):
    for at in range(0, UP * FR, 256):
        width = min(256, UP * FR - at)
        product = jnp.dot(hot_ref[...], x_ref[:, at : at + width], preferred_element_type=jnp.float32)
        lane = lax.broadcasted_iota(jnp.int32, (PAIR * SLOTS, width), 1)
        fine = lane // MG % UP
        total = jnp.zeros((PAIR * SLOTS, width), jnp.float32)
        for u in range(UP):
            rows = slice(u * PAIR * SLOTS, (u + 1) * PAIR * SLOTS)
            total = jnp.where(fine == u, product[rows, :], total)
        by_slope[:, at : at + width] = total
    whole = by_slope[...]
    high = whole.astype(jnp.bfloat16)
    low = (whole - high.astype(jnp.float32)).astype(jnp.bfloat16)
    series = jnp.dot(high, fold_ref[...], preferred_element_type=jnp.float32)
    series = series + jnp.dot(low, fold_ref[...], preferred_element_type=jnp.float32)
    at = 0
    for delay in range(MAXD + 1):
        first = first_slope(delay)
        size = USED - first
        for b in range(PAIR):
            rows = series[b * SLOTS + first : b * SLOTS + USED, :]
            if delay:
                rows = pltpu.roll(rows, 128 - delay, 1)
            stack[at : at + size, b * 128 : (b + 1) * 128] = rows
        at += size
    shifted = stack[...]
    high = shifted.astype(jnp.bfloat16)
    low = (shifted - high.astype(jnp.float32)).astype(jnp.bfloat16)
    series = jnp.dot(trial_ref[...], high, preferred_element_type=jnp.float32)
    series = series + jnp.dot(trial_ref[...], low, preferred_element_type=jnp.float32)
    series = series * scale_ref[0, 0]
    share = DM // POL
    for b in range(PAIR):
        turned = series[:, b * 128 : (b + 1) * 128].T
        for q in range(POL):
            out_ref[q, b] = turned[:TOUT, q * 32 : q * 32 + share]


def dedisperse(scale, normed, hot):
    vmem = pl.BlockSpec(memory_space=pltpu.VMEM)
    return pl.pallas_call(
        dedisperse_kernel,
        in_specs=[pl.BlockSpec(memory_space=pltpu.SMEM), vmem, vmem, vmem, vmem],
        out_specs=vmem,
        out_shape=jax.ShapeDtypeStruct((POL, PAIR, TOUT, DM // POL), jnp.float32),
        scratch_shapes=[
            pltpu.VMEM((PAIR * SLOTS, UP * FR), jnp.float32),
            pltpu.VMEM((STACK, PAIR * 128), jnp.float32),
        ],
        compiler_params=pltpu.CompilerParams(vmem_limit_bytes=VMEM_LIMIT),
        name="dedisperse",
    )(scale, normed, hot, jnp.asarray(fold_matrix()), jnp.asarray(trial_matrix()))


def slope_picker(slopes, mask):
    marked = jnp.where(mask != 0, slopes, -1).reshape(FREQ, UP).T
    marked = jnp.repeat(marked, PAIR, axis=1)[:, None, None, :]
    slope = jnp.arange(SLOTS, dtype=jnp.int32)[None, None, :, None]
    beam = jnp.arange(PAIR, dtype=jnp.int32)[None, :, None, None]
    column = jnp.arange(QUARTER, dtype=jnp.int32)[None, None, None, :]
    hot = (marked == slope) & (column % PAIR == beam)
    return hot.astype(jnp.bfloat16).reshape(UP * PAIR * SLOTS, QUARTER)


def on_device(voltages, gains, slopes, mask):
    me = lax.axis_index("pol")
    calibrated = calibrate(voltages[0, 0], gains[0, 0])
    tables = jnp.asarray(beam_tables())
    bank = jnp.asarray(bank_matrix())
    parts = []
    totals = 0.0
    for ahead in (2, 1, 3, 0):
        power, total = quarter_power((me + ahead) % POL, calibrated, tables, bank)
        totals = totals + total
        if ahead:
            power = lax.ppermute(power, "pol", [(i, (i + ahead) % POL) for i in range(POL)])
        parts.append(power)
    totals = lax.psum(totals, "pol")
    normed = normalize(totals, parts)
    turned = lax.all_to_all(normed.reshape(FREQ, PAIR, UP * FR), "freq", 0, 0, tiled=True)
    scale = lax.rsqrt(jnp.sum(mask).astype(jnp.float32)).reshape(1, 1)
    out = dedisperse(scale, turned.reshape(QUARTER, UP * FR), slope_picker(slopes, mask))
    out = lax.all_to_all(out, "pol", 0, 0, tiled=True)
    return out.reshape(POL * PAIR, TOUT, DM // POL)


def solution(mesh):
    placed = (P("freq", "pol", None, None, None), P("freq", "pol", None, None), P(), P())
    return jax.shard_map(
        on_device, mesh=mesh, in_specs=placed, out_specs=P("freq", None, "pol"), check_vma=False
    )
```

time: 319 us -> 107 us (0.34); the launches traced: 313 us -> 106 us
  waiting for transfers between devices: 134 us -> 20 us
  matrix products: 87.6 us -> 0 us
  local copies, waits for them, and re-layouts: 38.3 us -> 7.21 us
  Pallas kernels: 0 us -> 26.1 us
  other arithmetic: 23 us -> 1.74 us
  starting transfers between devices: 14.7 us -> 34.3 us
  blocking collectives: 0 us -> 16 us
  between operations: 14.4 us -> 0.97 us
    dot_general x56 -> x0, matrix products: 87.6 us -> none  [the longest x49 32.8 us: add_delay(): jnp.einsum('bct,cd->btd', window, picked, preferred_element_type=jnp.floa...]
    psum x1 -> x0, waiting for transfers between devices: 79.1 us -> none  [on_device(): summed = lax.psum(power_terms.astype(jnp.bfloat16), 'pol')]
    all_to_all x1, waiting for transfers between devices: 55.2 us -> 20 us  [on_device(): lax.all_to_all(normed.reshape(FREQ, PAIR, UP * FR), 'freq', 0, 0, tiled=T...]
    pallas_call x0 -> x7, Pallas kernels: none -> 26.1 us  [the longest x4 17.8 us: quarter_power(): pl.pallas_call(power_kernel, grid_spec=pltpu.PrefetchScalarGridSpec(num_s...]
    convert_element_type x4 -> x0, local copies, waits for them, and re-layouts: 20.8 us -> none  [the longest x2 11.8 us: on_device(): summed = lax.psum(power_terms.astype(jnp.bfloat16), 'pol')]
    ppermute x0 -> x3, starting transfers between devices: none -> 11.9 us  [on_device(): lax.ppermute(power, 'pol', [(i, (i + ahead) % POL) for i in range(POL)])]
    another operation x2 -> x0, other arithmetic: 9.75 us -> none
    psum x0 -> x1, blocking collectives: none -> 9.19 us  [on_device(): totals = lax.psum(totals, 'pol')]
  transfers between devices with their start and end apart: 2 -> 4, of which waited for: 2 -> 1; matrix products, arithmetic and copies ran while one was open for 0% -> 1% of each run, Pallas kernels for 0% -> 12%
where the time goes in v1:
time: 107 us; the launch traced here: 106 us
  starting transfers between devices  34.3 us (32%)
  Pallas kernels  26.1 us (24%)
  waiting for transfers between devices  20 us (19%)
  blocking collectives  16 us (15%)
  local copies, waits for them, and re-layouts  7.21 us (7%)
  other arithmetic  1.74 us (2%)
    all_to_all x1, starting transfers between devices, on_device(): lax.all_to_all(normed.reshape(FREQ, PAIR, UP * FR), 'freq', 0, 0, tiled=T...  22.4 us
    all_to_all x1, waiting for transfers between devices, on_device(): lax.all_to_all(normed.reshape(FREQ, PAIR, UP * FR), 'freq', 0, 0, tiled=T...  20 us
    pallas_call x4, Pallas kernels, quarter_power(): pl.pallas_call(power_kernel, grid_spec=pltpu.PrefetchScalarGridSpec(num_s...  17.8 us
    ppermute x3, starting transfers between devices, on_device(): lax.ppermute(power, 'pol', [(i, (i + ahead) % POL) for i in range(POL)])  11.9 us
    psum x1, blocking collectives, on_device(): totals = lax.psum(totals, 'pol')  9.19 us
    all_to_all x1, blocking collectives, on_device(): out = lax.all_to_all(out, 'pol', 0, 0, tiled=True)  6.81 us
    unnamed x20, local copies, waits for them, and re-layouts  5.26 us
    pallas_call x1, Pallas kernels, dedisperse(): pl.pallas_call(dedisperse_kernel, in_specs=[pl.BlockSpec(memory_space=plt...  3.24 us
  transfers between devices with their start and end apart: 4, of which 1 were waited for; matrix products, arithmetic and copies ran while one was open for 1% of the time, Pallas kernels for 12%

profile of v1, /device:TPU:1, one launch (start us, length us, event | category | flops | bytes accessed | tf_op | source)
XLA Modules:
  0.0 106.3 jit_solution(8147657586900028216)
XLA Ops:
  0.0 0.0 copy-start.1
  0.0 1.8 %copy-done.1 = bf16[1,1,1392,2,512]{4,3,2,1,0:T(2,128)(2,1)S(1)} copy-done((bf16[1,1,1392,2,512]{4,3,2,1,0:T(2,128)(2,1)S(1)}, bf16[1,1,1392,2,512]{4,3,2,1,0:T(2,128)(2,1)}, u32[]{:S(2)}) %copy-start.1) | copy-done | bytes 2850840
  1.8 0.0 copy-start.6
  1.8 0.7 copy-done.6
  2.5 0.0 copy-start
  2.5 3.0 %calibrate.1.cal_ref = bf16[1392,1024]{1,0:T(8,128)(2,1)S(1)} custom-call(bf16[11136,128]{1,0:T(8,128)(2,1)S(1)} %bitcast.16, f32[2,512]{1,0:T(2,128)S(1)} %bitcast.17), custom_call_target="tpu_custom_call" | custom-call | tf_op jit(solution)/shard_map/calibrate/pallas_call | solution.py:122
  5.5 0.0 copy-done
  5.5 4.6 %quarter_power.4 = (bf16[1152,256]{1,0:T(8,128)(2,1)}, f32[16,128]{1,0:T(8,128)S(1)}) custom-call(s32[1]{0:T(128)} %bitcast.1.q_ref, bf16[1392,1024]{1,0:T(8,128)(2,1)S(1)} %calibrate.1.cal_ref, bf16[4,1024,512]{2,1,0:T(8,128)(2,1)} %constant.58.clone.tab_ref, bf16[256,736]{1,0:T(8,128)(2,1)S(1)} %copy-done), custom_call_target="tpu_custom_call" | custom-call | flops 1459617792 | bytes 5000000 | tf_op jit(solution)/shard_map/quarter_power/pallas_call | solution.py:159
  10.2 5.5 %collective-permute-start = (bf16[1152,256]{1,0:T(8,128)(2,1)}, bf16[1152,256]{1,0:T(8,128)(2,1)}, u32[]{:S(2)}, u32[]{:S(2)}) collective-permute-start(bf16[1152,256]{1,0:T(8,128)(2,1)} %get-tuple-element.17), channel_id=1, source_target_pairs={{0,2},{1,3},{2,0},{3,1},{4,6},{5,7},{6,4},{7,5},{8,10},{9,11},{10,... | collective-permute-start | bytes 1769480 | tf_op jit(solution)/shard_map/ppermute | solution.py:287
  15.7 4.7 %quarter_power.5 = (bf16[1152,256]{1,0:T(8,128)(2,1)}, f32[16,128]{1,0:T(8,128)S(1)}) custom-call(s32[1]{0:T(128)} %bitcast.6.q_ref, bf16[1392,1024]{1,0:T(8,128)(2,1)S(1)} %calibrate.1.cal_ref, bf16[4,1024,512]{2,1,0:T(8,128)(2,1)} %constant.58.clone.tab_ref, bf16[256,736]{1,0:T(8,128)(2,1)S(1)} %copy-done), custom_call_target="tpu_custom_call" | custom-call | flops 1459617792 | bytes 5000000 | tf_op jit(solution)/shard_map/quarter_power/pallas_call | solution.py:159
  20.3 2.2 %collective-permute-start.1 = (bf16[1152,256]{1,0:T(8,128)(2,1)}, bf16[1152,256]{1,0:T(8,128)(2,1)}, u32[]{:S(2)}, u32[]{:S(2)}) collective-permute-start(bf16[1152,256]{1,0:T(8,128)(2,1)} %get-tuple-element.18), channel_id=1, source_target_pairs={{0,1},{1,2},{2,3},{3,0},{4,5},{5,6},{6,7},{7,4},{8,9},{9,10},{10,1... | collective-permute-start | bytes 1769480 | tf_op jit(solution)/shard_map/ppermute | solution.py:287
  22.5 4.6 %quarter_power.6 = (bf16[1152,256]{1,0:T(8,128)(2,1)}, f32[16,128]{1,0:T(8,128)S(1)}) custom-call(s32[1]{0:T(128)} %bitcast.7.q_ref, bf16[1392,1024]{1,0:T(8,128)(2,1)S(1)} %calibrate.1.cal_ref, bf16[4,1024,512]{2,1,0:T(8,128)(2,1)} %constant.58.clone.tab_ref, bf16[256,736]{1,0:T(8,128)(2,1)S(1)} %copy-done), custom_call_target="tpu_custom_call" | custom-call | flops 1459617792 | bytes 5000000 | tf_op jit(solution)/shard_map/quarter_power/pallas_call | solution.py:159
  27.2 4.3 %collective-permute-start.2 = (bf16[1152,256]{1,0:T(8,128)(2,1)}, bf16[1152,256]{1,0:T(8,128)(2,1)}, u32[]{:S(2)}, u32[]{:S(2)}) collective-permute-start(bf16[1152,256]{1,0:T(8,128)(2,1)} %get-tuple-element.19), channel_id=1, source_target_pairs={{0,3},{1,0},{2,1},{3,2},{4,7},{5,4},{6,5},{7,6},{8,11},{9,8},{10,9... | collective-permute-start | bytes 1769480 | tf_op jit(solution)/shard_map/ppermute | solution.py:287
  31.5 3.9 %quarter_power.7 = (bf16[1152,256]{1,0:T(8,128)(2,1)S(1)}, f32[16,128]{1,0:T(8,128)S(1)}) custom-call(s32[1]{0:T(128)} %bitcast.8.q_ref, bf16[1392,1024]{1,0:T(8,128)(2,1)S(1)} %calibrate.1.cal_ref, bf16[4,1024,512]{2,1,0:T(8,128)(2,1)} %constant.58.clone.tab_ref, bf16[256,736]{1,0:T(8,128)(2,1)S(1)} %copy-done), custom_call_target="tpu_custom_call" | custom-call | flops 1459617792 | bytes 5000000 | tf_op jit(solution)/shard_map/quarter_power/pallas_call | solution.py:159
  35.4 0.0 copy-start.2
  35.4 0.8 copy-done.2
  36.2 0.0 copy-start.7
  36.2 0.0 copy-start.8
  36.2 9.2 %psum.7.tot_ref = f32[16,128]{1,0:T(8,128)S(1)} all-reduce(f32[16,128]{1,0:T(8,128)S(1)} %add_add_fusion), channel_id=1, replica_groups=mesh['freq'=128,'pol'=4] {'pol'}, use_global_device_ids=true, to_apply=%region_1.2 | all-reduce | flops 2048 | bytes 16384 | tf_op jit(solution)/shard_map/psum | solution.py:289
  45.4 0.0 collective-permute-done.a_ref
  45.4 0.0 collective-permute-done.1.b_ref
  45.5 0.0 collective-permute-done.2.c_ref
  45.5 0.0 copy-start.3
  45.5 1.1 copy-done.3
  46.5 2.0 %normalize.1 = bf16[256,1152]{1,0:T(8,128)(2,1)S(1)} custom-call(f32[16,128]{1,0:T(8,128)S(1)} %psum.7.tot_ref, bf16[1152,256]{1,0:T(8,128)(2,1)} %collective-permute-done.a_ref, bf16[1152,256]{1,0:T(8,128)(2,1)} %collective-permute-done.1.b_ref, bf16[1152,256]{1,0:T(8,128)(2,1)} %collective-permute-done.2.c_ref, bf16[1152,256]{1,0:T(8,128)(2,1)S(1)} %copy-done.3), custom_call_target="tpu_custom_call" | custom-call | tf_op jit(solution)/shard_map/normalize/pallas_call | solution.py:202
  48.5 0.0 copy-start.4
  48.5 0.0 copy-start.5
  48.5 1.0 reshape.90
  49.6 22.4 %all-to-all-start = ((bf16[128,2,1152]{2,1,0:T(2,128)(2,1)}), bf16[128,2,1152]{2,1,0:T(2,128)(2,1)S(1)}, u32[]{:S(2)}, u32[]{:S(2)}) async-start(bf16[128,2,1152]{2,1,0:T(2,128)(2,1)} %reshape.90), calls=%async_computation | async-start | bytes 1179648 | tf_op jit(solution)/shard_map/all_to_all | solution.py:291
  72.0 0.0 copy-done.7
  72.0 0.0 copy-done.8
  72.0 0.6 compare_select_fusion
  72.6 0.1 reshape.92
  72.7 0.1 copy.11
  73.5 0.2 iota_compare_fusion
  73.7 0.2 and_convert_fusion
  73.9 20.0 %all-to-all-done = bf16[128,2,1152]{2,1,0:T(2,128)(2,1)S(1)} async-done(((bf16[128,2,1152]{2,1,0:T(2,128)(2,1)}), bf16[128,2,1152]{2,1,0:T(2,128)(2,1)S(1)}, u32[]{:S(2)}, u32[]{:S(2)}) %all-to-all-start) | async-done | bytes 589856 | tf_op jit(solution)/shard_map/all_to_all | solution.py:291
  93.9 0.2 reshape.91.x_ref
  94.1 0.0 copy-done.4
  94.2 0.0 copy-done.5
  94.2 3.2 %dedisperse.1 = f32[4,2,24,24]{3,2,1,0:T(8,128)S(1)} custom-call(f32[1,1]{1,0:T(1,128)} %bitcast.scale_ref, bf16[256,1152]{1,0:T(8,128)(2,1)S(1)} %reshape.91.x_ref, bf16[2048,256]{1,0:T(8,128)(2,1)S(1)} %bitcast.15, bf16[1152,128]{1,0:T(8,128)(2,1)S(1)} %copy-done.5, bf16[128,1736]{1,0:T(8,128)(2,1)S(1)} %copy-done.4), custom_call_target="tpu_custom_call" | custom-call | tf_op jit(solution)/shard_map/dedisperse/pallas_call | solution.py:252
  97.4 0.1 reshape.95
  97.5 6.8 %all_to_all.10 = f32[4,1,1152]{2,1,0:T(1,128)S(1)} all-to-all(f32[4,1,1152]{2,1,0:T(1,128)S(1)} %reshape.95), channel_id=1, replica_groups=mesh['freq'=128,'pol'=4] {'pol'}, dimensions={0} | all-to-all | bytes 36864 | tf_op jit(solution)/shard_map/all_to_all | solution.py:294
  104.4 0.5 broadcast.57
  104.9 0.7 reduce
  105.6 0.7 reshape.96
  (4 shorter events, 0.1 us)
Async XLA Ops:
  0.0 1.8 %copy-start.1 = (bf16[1,1,1392,2,512]{4,3,2,1,0:T(2,128)(2,1)S(1)}, bf16[1,1,1392,2,512]{4,3,2,1,0:T(2,128)(2,1)}, u32[]{:S(2)}) copy-start(bf16[1,1,1392,2,512]{4,3,2,1,0:T(2,128)(2,1)} %param.8) | copy-start | bytes 8552452
  1.8 0.7 copy-start.6
  2.5 3.0 %copy-start = (bf16[256,736]{1,0:T(8,128)(2,1)S(1)}, bf16[256,736]{1,0:T(8,128)(2,1)}, u32[]{:S(2)}) copy-start(bf16[256,736]{1,0:T(8,128)(2,1)} %constant.59.clone.bank_ref) | copy-start | bytes 1130500
  10.2 35.3 %collective-permute-start = (bf16[1152,256]{1,0:T(8,128)(2,1)}, bf16[1152,256]{1,0:T(8,128)(2,1)}, u32[]{:S(2)}, u32[]{:S(2)}) collective-permute-start(bf16[1152,256]{1,0:T(8,128)(2,1)} %get-tuple-element.17), channel_id=1, source_target_pairs={{0,2},{1,3},{2,0},{3,1},{4,6},{5,7},{6,4},{7,5},{8,10},{9,11},{10,... | collective-permute-start | bytes 1769480 | tf_op jit(solution)/shard_map/ppermute | solution.py:287
  20.3 25.1 %collective-permute-start.1 = (bf16[1152,256]{1,0:T(8,128)(2,1)}, bf16[1152,256]{1,0:T(8,128)(2,1)}, u32[]{:S(2)}, u32[]{:S(2)}) collective-permute-start(bf16[1152,256]{1,0:T(8,128)(2,1)} %get-tuple-element.18), channel_id=1, source_target_pairs={{0,1},{1,2},{2,3},{3,0},{4,5},{5,6},{6,7},{7,4},{8,9},{9,10},{10,1... | collective-permute-start | bytes 1769480 | tf_op jit(solution)/shard_map/ppermute | solution.py:287
  27.2 18.3 %collective-permute-start.2 = (bf16[1152,256]{1,0:T(8,128)(2,1)}, bf16[1152,256]{1,0:T(8,128)(2,1)}, u32[]{:S(2)}, u32[]{:S(2)}) collective-permute-start(bf16[1152,256]{1,0:T(8,128)(2,1)} %get-tuple-element.19), channel_id=1, source_target_pairs={{0,3},{1,0},{2,1},{3,2},{4,7},{5,4},{6,5},{7,6},{8,11},{9,8},{10,9... | collective-permute-start | bytes 1769480 | tf_op jit(solution)/shard_map/ppermute | solution.py:287
  35.4 0.8 copy-start.2
  36.2 35.7 %copy-start.7 = (s32[2048]{0:T(1024)S(1)}, s32[2048]{0:T(1024)}, u32[]{:S(2)}) copy-start(s32[2048]{0:T(1024)} %param.10) | copy-start | bytes 24580
  36.2 35.7 %copy-start.8 = (s32[2048]{0:T(1024)S(1)}, s32[2048]{0:T(1024)}, u32[]{:S(2)}) copy-start(s32[2048]{0:T(1024)} %param.11) | copy-start | bytes 24580
  45.5 1.1 %copy-start.3 = (bf16[1152,256]{1,0:T(8,128)(2,1)S(1)}, bf16[1152,256]{1,0:T(8,128)(2,1)}, u32[]{:S(2)}) copy-start(bf16[1152,256]{1,0:T(8,128)(2,1)} %copy-done.2) | copy-start | bytes 1769476
  48.5 45.7 %copy-start.4 = (bf16[128,1736]{1,0:T(8,128)(2,1)S(1)}, bf16[128,1736]{1,0:T(8,128)(2,1)}, u32[]{:S(2)}) copy-start(bf16[128,1736]{1,0:T(8,128)(2,1)} %constant.61.clone.trial_ref) | copy-start | bytes 1333252
  48.5 45.6 %copy-start.5 = (bf16[1152,128]{1,0:T(8,128)(2,1)S(1)}, bf16[1152,128]{1,0:T(8,128)(2,1)}, u32[]{:S(2)}) copy-start(bf16[1152,128]{1,0:T(8,128)(2,1)} %constant.60.clone.fold_ref) | copy-start | bytes 884740
  49.6 44.4 %all-to-all-start = ((bf16[128,2,1152]{2,1,0:T(2,128)(2,1)}), bf16[128,2,1152]{2,1,0:T(2,128)(2,1)S(1)}, u32[]{:S(2)}, u32[]{:S(2)}) async-start(bf16[128,2,1152]{2,1,0:T(2,128)(2,1)} %reshape.90), calls=%async_computation | async-start | bytes 1179648 | tf_op jit(solution)/shard_map/all_to_all | solution.py:291

commit v2 on v1

v2 whole, which is shorter than its diff:
```python
import functools
import math

import jax
import jax.numpy as jnp
import ml_dtypes
import numpy as np
from jax import lax
from jax.experimental import pallas as pl
from jax.experimental.pallas import tpu as pltpu
from jax.sharding import PartitionSpec as P

FEEDS = 512
BEAMS = 1024
UP = 16
TAPS = 16
DM = 96
MAXD = 48
TOUT = 24
FR = 72
TS = 1392
POL = 4
FREQ = 128
PAIR = BEAMS // (POL * FREQ)
QUARTER = FREQ * PAIR
MG = 8
BLOCKS = FR // MG
ROWS = UP * MG
SPAN = (MG - 1 + TAPS) * UP
SLOTS = 56
TILES = FEEDS // 128
KINDS = 2 * TILES
CHUNKS = ((0, 368), (368, 512), (880, 512))
CORES = 2
CHIPS = FREQ // CORES
HELD = CORES * PAIR
EPSILON = 1e-06
BF16 = ml_dtypes.bfloat16
VMEM_LIMIT = 32 * 1024 * 1024
WHOLE_VMEM = 58 * 1024 * 1024


@functools.lru_cache(None)
def beam_tables():
    n = np.arange(FEEDS)[:, None]
    f = np.arange(FREQ)[None, :]
    b = np.arange(PAIR)[:, None]
    scale = np.float32(1.0 / math.sqrt(FEEDS))
    out = []
    for q in range(POL):
        k = (f * (POL * PAIR) + q * PAIR + b).reshape(1, -1)
        angle = ((n * k) % BEAMS).astype(np.float32) * np.float32(2.0 * math.pi / BEAMS)
        c = np.cos(angle) * scale
        s = np.sin(angle) * scale
        top = np.concatenate([c, -s], axis=1)
        low = np.concatenate([s, c], axis=1)
        out.append(np.concatenate([top, low], axis=0))
    return np.stack(out).astype(BF16)


@functools.lru_cache(None)
def bank_matrix():
    length = TAPS * UP
    pos = np.arange(length, dtype=np.float64) + 0.5
    hann = 0.5 - 0.5 * np.cos(2.0 * math.pi * pos / length)
    taps = (np.sinc((pos - 0.5 * length) / UP) * hann).astype(np.float32).astype(BF16)
    taps = taps.astype(np.float64)
    real = np.zeros((2, UP, MG, SPAN))
    imag = np.zeros((2, UP, MG, SPAN))
    lag = np.arange(length)
    for u in range(UP):
        angle = 2.0 * math.pi * ((u * lag) % UP) / UP
        c, s = taps * np.cos(angle), taps * np.sin(angle)
        for m in range(MG):
            at = slice(m * UP, m * UP + length)
            real[0, u, m, at], imag[0, u, m, at] = c, s
            real[1, u, m, at], imag[1, u, m, at] = -s, c
    both = np.concatenate([real.reshape(2 * ROWS, SPAN), imag.reshape(2 * ROWS, SPAN)], axis=1)
    return both.astype(np.float32).astype(BF16)


@functools.lru_cache(None)
def fold_matrix():
    g, u, m8 = np.meshgrid(np.arange(BLOCKS), np.arange(UP), np.arange(MG), indexing="ij")
    m = (g * MG + m8).reshape(-1)
    return (m[:, None] == np.arange(128)[None, :]).astype(np.float32).astype(BF16)


def first_slope(delay):
    return 8 * (delay // 8)


@functools.lru_cache(None)
def trial_matrix():
    parts = []
    share = DM // POL
    for delay in range(MAXD + 1):
        slope = np.arange(first_slope(delay), SLOTS)
        block = np.zeros((POL * 32, slope.size), np.float32)
        for d in range(DM):
            block[(d // share) * 32 + d % share] = ((d * slope) // (DM - 1) == delay) & (slope <= MAXD)
        parts.append(block)
    full = np.concatenate(parts, axis=1)
    return full.astype(BF16)


STACK = sum(SLOTS - first_slope(delay) for delay in range(MAXD + 1))


VMEM = pl.BlockSpec(memory_space=pltpu.VMEM)
SMEM = pl.BlockSpec(memory_space=pltpu.SMEM)
HBM = pl.BlockSpec(memory_space=pltpu.HBM)
PARAMS = pltpu.CompilerParams(vmem_limit_bytes=VMEM_LIMIT)
WHOLE = pltpu.CompilerParams(vmem_limit_bytes=WHOLE_VMEM)


def by_kind(block):
    samples = block.shape[0] // KINDS
    lifted = block.reshape(samples // 8, 8, KINDS, 128)
    parts = [lifted[:, t] for t in range(8)]
    row = lax.broadcasted_iota(jnp.int32, parts[0].shape, 1)
    for bit in (1, 2, 4):
        low = (row & bit) == 0
        for t in range(8):
            if t & bit == 0:
                a, b = parts[t], parts[t + bit]
                parts[t] = jnp.where(low, a, pltpu.roll(b, bit, 1))
                parts[t + bit] = jnp.where(low, pltpu.roll(a, 8 - bit, 1), b)
    return [part.reshape(samples, 128) for part in parts]


def calibrate_rows(v_ref, g_ref, cal_ref, start, size):
    kinds = by_kind(v_ref[start * KINDS : (start + size) * KINDS, :].astype(jnp.float32))
    rows = slice(start, start + size)
    for j in range(TILES):
        re, im = kinds[2 * j], kinds[2 * j + 1]
        lanes = slice(j * 128, (j + 1) * 128)
        gr = g_ref[0:1, lanes]
        gi = g_ref[1:2, lanes]
        cal_ref[rows, lanes] = (re * gr - im * gi).astype(jnp.bfloat16)
        lanes = slice(FEEDS + j * 128, FEEDS + (j + 1) * 128)
        cal_ref[rows, lanes] = (re * gi + im * gr).astype(jnp.bfloat16)


def form(cal_ref, tab_ref, formed, start, size):
    rows = slice(start, start + size)
    formed[rows, :] = jnp.dot(
        cal_ref[rows, :], tab_ref[...], preferred_element_type=jnp.float32
    ).astype(jnp.bfloat16)


def filter_power(bank_ref, formed, out_ref, tot_ref):
    total = jnp.zeros((ROWS, QUARTER), jnp.float32)
    for g in range(BLOCKS):
        rows = slice(g * ROWS, g * ROWS + SPAN)
        both = jnp.concatenate([formed[rows, :QUARTER], formed[rows, QUARTER:]], axis=0)
        fine = jnp.dot(bank_ref[...], both, preferred_element_type=jnp.float32)
        re, im = fine[:ROWS], fine[ROWS:]
        power = (re * re + im * im).astype(jnp.bfloat16)
        out_ref[g * ROWS : (g + 1) * ROWS, :] = power
        total = total + power.astype(jnp.float32)
    for u in range(UP):
        part = total[u * MG : (u + 1) * MG]
        tot_ref[u : u + 1, :] = jnp.broadcast_to(jnp.sum(part, keepdims=True), (1, 128))


def row_copies(source, target, sems, scale=1):
    copies = []
    for i, (start, size) in enumerate(CHUNKS):
        rows = pl.ds(start * scale, size * scale)
        copies.append(pltpu.make_async_copy(source.at[rows, :], target.at[rows, :], sems.at[i]))
    return copies


def lead_kernel(
    q_ref, v_hbm, g_ref, tab_hbm, bank_ref, out_ref, tot_ref, cal_hbm, v_ref, tab_ref, cal_ref, formed, sems
):
    loads = row_copies(v_hbm, v_ref, sems.at[0], KINDS)
    stores = row_copies(cal_ref, cal_hbm, sems.at[1])
    table = pltpu.make_async_copy(tab_hbm.at[q_ref[0]], tab_ref, sems.at[2, 0])
    for copy in loads[:1] + [table] + loads[1:]:
        copy.start()
    for i in range(len(CHUNKS) + 1):
        if i < len(CHUNKS):
            loads[i].wait()
            calibrate_rows(v_ref, g_ref, cal_ref, *CHUNKS[i])
            stores[i].start()
        if i == 0:
            table.wait()
        else:
            form(cal_ref, tab_ref, formed, *CHUNKS[i - 1])
    filter_power(bank_ref, formed, out_ref, tot_ref)
    for copy in stores:
        copy.wait()


REST = POL - 1


def rest_kernel(q_ref, cal_hbm, tab_hbm, bank_ref, *refs):
    out_hbms, tot_ref = refs[:REST], refs[REST]
    cal_ref, tab_ref, formed, out_ref, tot_parts, cal_sems, tab_sems, out_sems = refs[REST + 1 :]
    loads = row_copies(cal_hbm, cal_ref, cal_sems)
    tables = [
        pltpu.make_async_copy(tab_hbm.at[q_ref[n]], tab_ref.at[n], tab_sems.at[n]) for n in range(REST)
    ]
    for copy in tables[:1] + loads + tables[1:]:
        copy.start()
    stores = []
    for n in range(REST):
        tables[n].wait()
        for i, chunk in enumerate(CHUNKS):
            if n == 0:
                loads[i].wait()
            form(cal_ref, tab_ref.at[n], formed.at[n], *chunk)
        filter_power(bank_ref, formed.at[n], out_ref.at[n], tot_parts.at[n])
        stores.append(pltpu.make_async_copy(out_ref.at[n], out_hbms[n], out_sems.at[n]))
        stores[-1].start()
    tot_ref[...] = tot_parts[0] + tot_parts[1] + tot_parts[2]
    for copy in stores:
        copy.wait()


POWER = jax.ShapeDtypeStruct((UP * FR, QUARTER), jnp.bfloat16)
TOTAL = jax.ShapeDtypeStruct((UP, 128), jnp.float32)
def lead_power(index, voltages, gains, tables, bank):
    flat = voltages.reshape(TS, 2, TILES, 128).transpose(0, 2, 1, 3).reshape(TS * KINDS, 128)
    return pl.pallas_call(
        lead_kernel,
        in_specs=[SMEM, HBM, VMEM, HBM, VMEM],
        out_specs=[VMEM, VMEM, HBM],
        out_shape=[POWER, TOTAL, jax.ShapeDtypeStruct((TS, 2 * FEEDS), jnp.bfloat16)],
        scratch_shapes=[
            pltpu.VMEM((TS * KINDS, 128), jnp.bfloat16),
            pltpu.VMEM((2 * FEEDS, 2 * QUARTER), jnp.bfloat16),
            pltpu.VMEM((TS, 2 * FEEDS), jnp.bfloat16),
            pltpu.VMEM((TS, 2 * QUARTER), jnp.bfloat16),
            pltpu.SemaphoreType.DMA((3, len(CHUNKS))),
        ],
        compiler_params=WHOLE,
        cost_estimate=pl.CostEstimate(flops=3_000_000_000, bytes_accessed=8_000_000, transcendentals=0),
        name="lead_power",
    )(index.reshape(1), flat, gains, tables, bank)


def rest_powers(indices, calibrated, tables, bank):
    return pl.pallas_call(
        rest_kernel,
        in_specs=[SMEM, HBM, HBM, VMEM],
        out_specs=[HBM] * REST + [VMEM],
        out_shape=[POWER] * REST + [TOTAL],
        scratch_shapes=[
            pltpu.VMEM((TS, 2 * FEEDS), jnp.bfloat16),
            pltpu.VMEM((REST, 2 * FEEDS, 2 * QUARTER), jnp.bfloat16),
            pltpu.VMEM((REST, TS, 2 * QUARTER), jnp.bfloat16),
            pltpu.VMEM((REST, UP * FR, QUARTER), jnp.bfloat16),
            pltpu.VMEM((REST, UP, 128), jnp.float32),
            pltpu.SemaphoreType.DMA((len(CHUNKS),)),
            pltpu.SemaphoreType.DMA((REST,)),
            pltpu.SemaphoreType.DMA((REST,)),
        ],
        compiler_params=WHOLE,
        cost_estimate=pl.CostEstimate(flops=9_000_000_000, bytes_accessed=8_000_000, transcendentals=0),
        name="rest_powers",
    )(jnp.stack(indices), calibrated, tables, bank)


def normalize_kernel(tot_ref, a_ref, b_ref, c_ref, d_ref, out_ref, inverse):
    for u in range(UP):
        mean = tot_ref[u : u + 1, :] * (1.0 / (BEAMS * FR))
        inverse[u * MG : (u + 1) * MG, :] = jnp.broadcast_to(1.0 / (mean + EPSILON), (MG, 128))
    scale = inverse[...]
    for g in range(BLOCKS):
        rows = slice(g * ROWS, (g + 1) * ROWS)
        for b in range(PAIR):
            lanes = slice(b * FREQ, (b + 1) * FREQ)
            total = d_ref[rows, lanes].astype(jnp.float32)
            for ref in (a_ref, b_ref, c_ref):
                total = total + ref[rows, lanes].astype(jnp.float32)
            summed = total.astype(jnp.bfloat16).astype(jnp.float32)
            normed = summed * scale - 1.0
            at = b * UP * FR + g * ROWS
            out_ref[:, at : at + ROWS] = normed.T.astype(jnp.bfloat16)


def normalize(totals, parts):
    return pl.pallas_call(
        normalize_kernel,
        in_specs=[VMEM] * (1 + POL),
        out_specs=VMEM,
        out_shape=jax.ShapeDtypeStruct((FREQ, PAIR * UP * FR), jnp.bfloat16),
        scratch_shapes=[pltpu.VMEM((ROWS, 128), jnp.float32)],
        compiler_params=PARAMS,
        name="normalize",
    )(totals, *parts)


def dedisperse_kernel(scale_ref, x_ref, hot_ref, fold_ref, trial_ref, out_ref, by_slope, stack):
    picked = CORES * SLOTS
    series = [None] * HELD
    for b in range(PAIR):
        for at in range(0, UP * FR, 256):
            width = min(256, UP * FR - at)
            start = b * UP * FR + at
            values = x_ref[:, start : start + width]
            fine = lax.broadcasted_iota(jnp.int32, values.shape, 1) // MG
            empty = jnp.zeros_like(values)
            even = jnp.where(fine % 2 == 0, values, empty)
            odd = jnp.where(fine % 2 == 0, empty, values)
            both = jnp.concatenate([even, odd], axis=0)
            product = jnp.dot(hot_ref[...], both, preferred_element_type=jnp.float32)
            couple = lax.broadcasted_iota(jnp.int32, (picked, width), 1) // (2 * MG) % (UP // 2)
            total = product[:picked, :]
            for n in range(1, UP // 2):
                total = jnp.where(couple == n, product[n * picked : (n + 1) * picked, :], total)
            by_slope[b, :, at : at + width] = total
        whole = by_slope[b]
        high = whole.astype(jnp.bfloat16)
        low = (whole - high.astype(jnp.float32)).astype(jnp.bfloat16)
        folded = jnp.dot(high, fold_ref[...], preferred_element_type=jnp.float32)
        folded = folded + jnp.dot(low, fold_ref[...], preferred_element_type=jnp.float32)
        for core in range(CORES):
            series[core * PAIR + b] = folded[core * SLOTS : (core + 1) * SLOTS]
    lane = lax.broadcasted_iota(jnp.int32, (SLOTS, 128), 1) // 32
    at = 0
    for delay in range(MAXD + 1):
        first = first_slope(delay)
        size = SLOTS - first
        packed = jnp.zeros((size, 128), jnp.float32)
        for b in range(HELD):
            rows = series[b][first:, :]
            shift = (32 * b - delay) % 128
            rows = pltpu.roll(rows, shift, 1) if shift else rows
            packed = jnp.where(lane[:size] == b, rows, packed)
        stack[at : at + size, :] = packed
        at += size
    shifted = stack[...]
    high = shifted.astype(jnp.bfloat16)
    low = (shifted - high.astype(jnp.float32)).astype(jnp.bfloat16)
    result = jnp.dot(trial_ref[...], high, preferred_element_type=jnp.float32)
    result = result + jnp.dot(trial_ref[...], low, preferred_element_type=jnp.float32)
    turned = (result * scale_ref[0, 0]).T
    for q in range(POL):
        rolled = pltpu.roll(turned, 128 - 32 * q, 1) if q else turned
        for core in range(CORES):
            for b in range(PAIR):
                start = 32 * (core * PAIR + b)
                out_ref[core * POL + q, b] = rolled[start : start + TOUT]


def dedisperse(scale, normed, hot):
    return pl.pallas_call(
        dedisperse_kernel,
        in_specs=[SMEM, VMEM, VMEM, VMEM, VMEM],
        out_specs=VMEM,
        out_shape=jax.ShapeDtypeStruct((CORES * POL, PAIR, TOUT, 128), jnp.float32),
        scratch_shapes=[
            pltpu.VMEM((PAIR, CORES * SLOTS, UP * FR), jnp.float32),
            pltpu.VMEM((STACK, 128), jnp.float32),
        ],
        compiler_params=PARAMS,
        name="dedisperse",
    )(scale, normed, hot, jnp.asarray(fold_matrix()), jnp.asarray(trial_matrix()))


def slope_picker(slopes, mask, core):
    marked = jnp.where(mask != 0, slopes, -1).reshape(CHIPS, CORES, UP)
    marked = lax.dynamic_index_in_dim(marked, core, 1, keepdims=False).T.reshape(UP // 2, 2 * CHIPS)
    marked = jnp.repeat(marked, CORES, axis=1)[:, None, None, :]
    slope = jnp.arange(SLOTS, dtype=jnp.int32)[None, None, :, None]
    own = jnp.arange(CORES, dtype=jnp.int32)[None, :, None, None]
    column = jnp.arange(2 * FREQ, dtype=jnp.int32)[None, None, None, :]
    hot = (marked == slope) & (column % CORES == own)
    return hot.astype(jnp.bfloat16).reshape(UP // 2 * CORES * SLOTS, 2 * FREQ)


def on_device(voltages, gains, slopes, mask):
    me = lax.axis_index("pol")
    core = lax.axis_index("freq") % CORES
    tables = jnp.asarray(beam_tables())
    bank = jnp.asarray(bank_matrix())
    index = [(me + ahead) % POL for ahead in range(POL)]

    def send(power, ahead):
        return lax.ppermute(power, "pol", [(i, (i + ahead) % POL) for i in range(POL)])

    far, far_total, calibrated = lead_power(index[2], voltages[0, 0], gains[0, 0], tables, bank)
    far = send(far, 2)
    right, left, own, rest_total = rest_powers([index[1], index[3], index[0]], calibrated, tables, bank)
    parts = [far, send(right, 1), send(left, 3), own]
    normed = normalize(lax.psum(far_total + rest_total, "pol"), parts)
    alike = [[CORES * chip + c for chip in range(CHIPS)] for c in range(CORES)]
    turned = lax.all_to_all(
        normed.reshape(CHIPS, CORES, PAIR * UP * FR), "freq", 0, 0, tiled=True, axis_index_groups=alike
    )
    scale = lax.rsqrt(jnp.sum(mask).astype(jnp.float32)).reshape(1, 1)
    out = dedisperse(scale, turned.reshape(FREQ, PAIR * UP * FR), slope_picker(slopes, mask, core))
    near = [
        [(CORES * chip + c) * POL + q for c in range(CORES) for q in range(POL)] for chip in range(CHIPS)
    ]
    out = lax.all_to_all(out, ("freq", "pol"), 0, 0, tiled=True, axis_index_groups=near)
    out = out[:POL] + out[POL:]
    return out.reshape(POL * PAIR, TOUT, 128)[:, :, : DM // POL]


def solution(mesh):
    placed = (P("freq", "pol", None, None, None), P("freq", "pol", None, None), P(), P())
    return jax.shard_map(
        on_device, mesh=mesh, in_specs=placed, out_specs=P("freq", None, "pol"), check_vma=False
    )
```

time: 107 us -> 111 us (1.037)
  blocking collectives: 16 us -> 39 us
  starting transfers between devices: 34.3 us -> 27.2 us
  waiting for transfers between devices: 20 us -> 13.1 us
  local copies, waits for them, and re-layouts: 7.21 us -> 2.86 us
  Pallas kernels: 26.1 us -> 24.6 us
    psum x1, blocking collectives: 9.19 us -> 22.2 us  [on_device(): normed = normalize(lax.psum(far_total + rest_total, 'pol'), parts)]
    all_to_all x1, blocking collectives: 6.81 us -> 16.8 us  [on_device(): lax.all_to_all(out, ('freq', 'pol'), 0, 0, tiled=True, axis_index_groups=...]
    all_to_all x1, waiting for transfers between devices: 20 us -> 13.1 us  [on_device(): lax.all_to_all(normed.reshape(CHIPS, CORES, PAIR * UP * FR), 'freq', 0, 0...]
    all_to_all x1, starting transfers between devices: 22.4 us -> 16.4 us  [on_device(): lax.all_to_all(normed.reshape(CHIPS, CORES, PAIR * UP * FR), 'freq', 0, 0...]
    unnamed x20 -> x14, local copies, waits for them, and re-layouts: 5.26 us -> 1.09 us
    pallas_call x7 -> x4, Pallas kernels: 26.1 us -> 24.6 us  [the longest x1 12.7 us: rest_powers(): pl.pallas_call(rest_kernel, in_specs=[SMEM, HBM, HBM, VMEM], out_specs=[H...]
    add x1 -> x2, other arithmetic: 0.01 us -> 1.35 us  [the longest x1 0.7 us: on_device(): normed = normalize(lax.psum(far_total + rest_total, 'pol'), parts)]
    ppermute x3, starting transfers between devices: 11.9 us -> 10.8 us  [send(): lax.ppermute(power, 'pol', [(i, (i + ahead) % POL) for i in range(POL)])]
  transfers between devices with their start and end apart: 4 -> 4, of which waited for: 1 -> 1; matrix products, arithmetic and copies ran while one was open for 1% -> 2% of each run, Pallas kernels for 12% -> 0%
where the time goes in v2:
time: 111 us
  blocking collectives  39 us (35%)
  starting transfers between devices  27.2 us (25%)
  Pallas kernels  24.6 us (22%)
  waiting for transfers between devices  13.1 us (12%)
  local copies, waits for them, and re-layouts  2.86 us (3%)
  other arithmetic  2.83 us (3%)
    psum x1, blocking collectives, on_device(): normed = normalize(lax.psum(far_total + rest_total, 'pol'), parts)  22.2 us
    all_to_all x1, blocking collectives, on_device(): lax.all_to_all(out, ('freq', 'pol'), 0, 0, tiled=True, axis_index_groups=...  16.8 us
    all_to_all x1, starting transfers between devices, on_device(): lax.all_to_all(normed.reshape(CHIPS, CORES, PAIR * UP * FR), 'freq', 0, 0...  16.4 us
    all_to_all x1, waiting for transfers between devices, on_device(): lax.all_to_all(normed.reshape(CHIPS, CORES, PAIR * UP * FR), 'freq', 0, 0...  13.1 us
    pallas_call x1, Pallas kernels, rest_powers(): pl.pallas_call(rest_kernel, in_specs=[SMEM, HBM, HBM, VMEM], out_specs=[H...  12.7 us
    ppermute x3, starting transfers between devices, send(): lax.ppermute(power, 'pol', [(i, (i + ahead) % POL) for i in range(POL)])  10.8 us
    pallas_call x1, Pallas kernels, lead_power(): pl.pallas_call(lead_kernel, in_specs=[SMEM, HBM, VMEM, HBM, VMEM], out_sp...  8.39 us
    pallas_call x1, Pallas kernels, dedisperse(): pl.pallas_call(dedisperse_kernel, in_specs=[SMEM, VMEM, VMEM, VMEM, VMEM]...  2.93 us
  transfers between devices with their start and end apart: 4, of which 1 were waited for; matrix products, arithmetic and copies ran while one was open for 2% of the time, Pallas kernels for 0%

profile of v2, /device:TPU:1, one launch (start us, length us, event | category | flops | bytes accessed | tf_op | source)
XLA Modules:
  0.0 110.5 jit_solution(1621536523909454738)
XLA Ops:
  0.0 0.7 pad_add_fusion.q_ref
  0.7 8.4 %lead_power.1 = (bf16[1152,256]{1,0:T(8,128)(2,1)}, f32[16,128]{1,0:T(8,128)}, bf16[1392,1024]{1,0:T(8,128)(2,1)}) custom-call(s32[1]{0:T(128)} %bitcast.1.q_ref, bf16[11136,128]{1,0:T(8,128)(2,1)} %bitcast.22, f32[2,512]{1,0:T(2,128)} %bitcast.23, bf16[4,1024,512]{2,1,0:T(8,128)(2,1)} %constant.71.clone.tab_hbm, bf16[256,736]{1,0:T(8,128)(2,1)} %constant.72.clone.bank_ref), custom_call_target="tpu_custom_call" | custom-call | flops 3000000000 | bytes 8000000 | tf_op jit(solution)/shard_map/lead_power/pallas_call | solution.py:228
  9.1 0.0 copy-start.6
  9.1 0.0 copy-start.5
  9.1 12.7 %rest_powers.1 = (bf16[1152,256]{1,0:T(8,128)(2,1)}, bf16[1152,256]{1,0:T(8,128)(2,1)}, bf16[1152,256]{1,0:T(8,128)(2,1)}, f32[16,128]{1,0:T(8,128)}) custom-call(s32[3]{0:T(128)} %pad_add_fusion.q_ref, bf16[1392,1024]{1,0:T(8,128)(2,1)} %get-tuple-element.13.cal_hbm, bf16[4,1024,512]{2,1,0:T(8,128)(2,1)} %constant.71.clone.tab_hbm, ...), custom_call_target="tpu_custom_call" | custom-call | flops 8999999488 | bytes 8000000 | tf_op jit(solution)/shard_map/rest_powers/pallas_call | solution.py:247
  21.8 0.0 copy-start.3
  21.8 0.0 copy-start.4
  21.8 3.9 %collective-permute-start.1 = (bf16[1152,256]{1,0:T(8,128)(2,1)}, bf16[1152,256]{1,0:T(8,128)(2,1)S(1)}, u32[]{:S(2)}, u32[]{:S(2)}) collective-permute-start(bf16[1152,256]{1,0:T(8,128)(2,1)} %get-tuple-element.16), channel_id=1, source_target_pairs={{0,1},{1,2},{2,3},{3,0},{4,5},{5,6},{6,7},{7,4},{8,9},{9,10},{10,1... | collective-permute-start | bytes 1769480 | tf_op jit(solution)/shard_map/ppermute | solution.py:385
  25.8 3.2 %collective-permute-start.2 = (bf16[1152,256]{1,0:T(8,128)(2,1)}, bf16[1152,256]{1,0:T(8,128)(2,1)S(1)}, u32[]{:S(2)}, u32[]{:S(2)}) collective-permute-start(bf16[1152,256]{1,0:T(8,128)(2,1)} %get-tuple-element.17), channel_id=1, source_target_pairs={{0,3},{1,0},{2,1},{3,2},{4,7},{5,4},{6,5},{7,6},{8,11},{9,8},{10,9... | collective-permute-start | bytes 1769480 | tf_op jit(solution)/shard_map/ppermute | solution.py:385
  29.0 0.0 copy-done.6
  29.0 3.6 %collective-permute-start = (bf16[1152,256]{1,0:T(8,128)(2,1)S(1)}, bf16[1152,256]{1,0:T(8,128)(2,1)S(1)}, u32[]{:S(2)}, u32[]{:S(2)}) collective-permute-start(bf16[1152,256]{1,0:T(8,128)(2,1)S(1)} %copy-done.6), channel_id=1, source_target_pairs={{0,2},{1,3},{2,0},{3,1},{4,6},{5,7},{6,4},{7,5},{8,10},{9,11},{10,... | collective-permute-start | bytes 1769480 | tf_op jit(solution)/shard_map/ppermute | solution.py:385
  32.6 0.0 copy-done.5
  32.6 0.7 add.55
  33.4 22.2 %psum.7.tot_ref = f32[16,128]{1,0:T(8,128)S(1)} all-reduce(f32[16,128]{1,0:T(8,128)S(1)} %add.55), channel_id=1, replica_groups=mesh['freq'=128,'pol'=4] {'pol'}, use_global_device_ids=true, to_apply=%region_1.2 | all-reduce | flops 2048 | bytes 16384 | tf_op jit(solution)/shard_map/psum | solution.py:391
  55.6 0.0 collective-permute-done.1.b_ref
  55.6 0.0 collective-permute-done.2.c_ref
  55.6 0.0 collective-permute-done.a_ref
  55.6 0.0 copy-start
  55.6 1.1 copy-done
  56.7 0.5 normalize.1
  57.2 0.0 copy-start.1
  57.2 0.0 copy-start.2
  57.2 1.0 reshape.81
  58.3 16.4 %all-to-all-start = ((bf16[64,2,2304]{2,1,0:T(2,128)(2,1)}), bf16[64,2,2304]{2,1,0:T(2,128)(2,1)S(1)}, u32[]{:S(2)}, u32[]{:S(2)}) async-start(bf16[64,2,2304]{2,1,0:T(2,128)(2,1)} %reshape.81), calls=%async_computation | async-start | bytes 1179648 | tf_op jit(solution)/shard_map/all_to_all | solution.py:393
  74.7 0.0 copy-done.3
  74.7 0.0 copy-done.4
  74.7 0.6 compare_select_fusion
  75.3 0.1 reshape.83
  75.5 0.1 copy.16
  75.6 0.1 reshape.84
  75.7 0.1 copy.17
  75.8 0.1 copy.18
  76.6 0.1 iota_compare_fusion
  76.7 0.1 and_convert_fusion
  76.8 13.1 %all-to-all-done = bf16[64,2,2304]{2,1,0:T(2,128)(2,1)S(1)} async-done(((bf16[64,2,2304]{2,1,0:T(2,128)(2,1)}), bf16[64,2,2304]{2,1,0:T(2,128)(2,1)S(1)}, u32[]{:S(2)}, u32[]{:S(2)}) %all-to-all-start) | async-done | bytes 589856 | tf_op jit(solution)/shard_map/all_to_all | solution.py:393
  89.9 0.2 reshape.82.x_ref
  90.1 0.0 copy-done.1
  90.2 0.0 copy-done.2
  90.2 2.9 %dedisperse.1 = f32[8,2,24,128]{3,2,1,0:T(8,128)S(1)} custom-call(f32[1,1]{1,0:T(1,128)} %bitcast.scale_ref, bf16[128,2304]{1,0:T(8,128)(2,1)S(1)} %reshape.82.x_ref, bf16[896,256]{1,0:T(8,128)(2,1)S(1)} %bitcast.18, bf16[1152,128]{1,0:T(8,128)(2,1)S(1)} %copy-done.2, bf16[128,1736]{1,0:T(8,128)(2,1)S(1)} %copy-done.1), custom_call_target="tpu_custom_call" | custom-call | tf_op jit(solution)/shard_map/dedisperse/pallas_call | solution.py:352
  93.1 16.8 %all_to_all.10 = f32[8,2,24,128]{3,2,1,0:T(8,128)S(1)} all-to-all(f32[8,2,24,128]{3,2,1,0:T(8,128)S(1)} %dedisperse.1), channel_id=1, replica_groups={{0,1,2,3,4,5,6,7},{8,9,10,11,12,13,14,15},{16,17,18,19,20,21,22,23},{24..., dimensions={0} | all-to-all | bytes 393216 | tf_op jit(solution)/shard_map/all_to_all | solution.py:401
  109.9 0.7 slice_add_fusion
  (4 shorter events, 0.1 us)
Async XLA Ops:
  9.1 19.9 %copy-start.6 = (bf16[1152,256]{1,0:T(8,128)(2,1)S(1)}, bf16[1152,256]{1,0:T(8,128)(2,1)}, u32[]{:S(2)}) copy-start(bf16[1152,256]{1,0:T(8,128)(2,1)} %get-tuple-element.15) | copy-start | bytes 1769476
  9.1 23.6 %copy-start.5 = (f32[16,128]{1,0:T(8,128)S(1)}, f32[16,128]{1,0:T(8,128)}, u32[]{:S(2)}) copy-start(f32[16,128]{1,0:T(8,128)} %get-tuple-element.12) | copy-start | bytes 24580
  21.8 52.9 %copy-start.3 = (s32[2048]{0:T(1024)S(1)}, s32[2048]{0:T(1024)}, u32[]{:S(2)}) copy-start(s32[2048]{0:T(1024)} %param.10) | copy-start | bytes 24580
  21.8 52.9 %copy-start.4 = (s32[2048]{0:T(1024)S(1)}, s32[2048]{0:T(1024)}, u32[]{:S(2)}) copy-start(s32[2048]{0:T(1024)} %param.11) | copy-start | bytes 24580
  21.8 33.7 %collective-permute-start.1 = (bf16[1152,256]{1,0:T(8,128)(2,1)}, bf16[1152,256]{1,0:T(8,128)(2,1)S(1)}, u32[]{:S(2)}, u32[]{:S(2)}) collective-permute-start(bf16[1152,256]{1,0:T(8,128)(2,1)} %get-tuple-element.16), channel_id=1, source_target_pairs={{0,1},{1,2},{2,3},{3,0},{4,5},{5,6},{6,7},{7,4},{8,9},{9,10},{10,1... | collective-permute-start | bytes 1769480 | tf_op jit(solution)/shard_map/ppermute | solution.py:385
  25.8 29.8 %collective-permute-start.2 = (bf16[1152,256]{1,0:T(8,128)(2,1)}, bf16[1152,256]{1,0:T(8,128)(2,1)S(1)}, u32[]{:S(2)}, u32[]{:S(2)}) collective-permute-start(bf16[1152,256]{1,0:T(8,128)(2,1)} %get-tuple-element.17), channel_id=1, source_target_pairs={{0,3},{1,0},{2,1},{3,2},{4,7},{5,4},{6,5},{7,6},{8,11},{9,8},{10,9... | collective-permute-start | bytes 1769480 | tf_op jit(solution)/shard_map/ppermute | solution.py:385
  29.0 26.6 %collective-permute-start = (bf16[1152,256]{1,0:T(8,128)(2,1)S(1)}, bf16[1152,256]{1,0:T(8,128)(2,1)S(1)}, u32[]{:S(2)}, u32[]{:S(2)}) collective-permute-start(bf16[1152,256]{1,0:T(8,128)(2,1)S(1)} %copy-done.6), channel_id=1, source_target_pairs={{0,2},{1,3},{2,0},{3,1},{4,6},{5,7},{6,4},{7,5},{8,10},{9,11},{10,... | collective-permute-start | bytes 1769480 | tf_op jit(solution)/shard_map/ppermute | solution.py:385
  55.6 1.1 copy-start
  57.2 32.9 %copy-start.1 = (bf16[128,1736]{1,0:T(8,128)(2,1)S(1)}, bf16[128,1736]{1,0:T(8,128)(2,1)}, u32[]{:S(2)}) copy-start(bf16[128,1736]{1,0:T(8,128)(2,1)} %constant.74.clone.trial_ref) | copy-start | bytes 1333252
  57.2 32.9 %copy-start.2 = (bf16[1152,128]{1,0:T(8,128)(2,1)S(1)}, bf16[1152,128]{1,0:T(8,128)(2,1)}, u32[]{:S(2)}) copy-start(bf16[1152,128]{1,0:T(8,128)(2,1)} %constant.73.clone.fold_ref) | copy-start | bytes 884740
  58.3 31.7 %all-to-all-start = ((bf16[64,2,2304]{2,1,0:T(2,128)(2,1)}), bf16[64,2,2304]{2,1,0:T(2,128)(2,1)S(1)}, u32[]{:S(2)}, u32[]{:S(2)}) async-start(bf16[64,2,2304]{2,1,0:T(2,128)(2,1)} %reshape.81), calls=%async_computation | async-start | bytes 1179648 | tf_op jit(solution)/shard_map/all_to_all | solution.py:393

commit v3 on v2

--- a/solution.py
+++ b/solution.py
@@ -30,14 +30,14 @@
 SLOTS = 56
 TILES = FEEDS // 128
 KINDS = 2 * TILES
-CHUNKS = ((0, 368), (368, 512), (880, 512))
+CHUNKS = ((0, 464), (464, 464), (928, 464))
 CORES = 2
 CHIPS = FREQ // CORES
 HELD = CORES * PAIR
 EPSILON = 1e-06
 BF16 = ml_dtypes.bfloat16
 VMEM_LIMIT = 32 * 1024 * 1024
-WHOLE_VMEM = 58 * 1024 * 1024
+WHOLE_VMEM = 48 * 1024 * 1024
 
 
 @functools.lru_cache(None)
@@ -164,104 +164,61 @@
         tot_ref[u : u + 1, :] = jnp.broadcast_to(jnp.sum(part, keepdims=True), (1, 128))
 
 
-def row_copies(source, target, sems, scale=1):
-    copies = []
-    for i, (start, size) in enumerate(CHUNKS):
-        rows = pl.ds(start * scale, size * scale)
-        copies.append(pltpu.make_async_copy(source.at[rows, :], target.at[rows, :], sems.at[i]))
-    return copies
-
-
-def lead_kernel(
-    q_ref, v_hbm, g_ref, tab_hbm, bank_ref, out_ref, tot_ref, cal_hbm, v_ref, tab_ref, cal_ref, formed, sems
-):
-    loads = row_copies(v_hbm, v_ref, sems.at[0], KINDS)
-    stores = row_copies(cal_ref, cal_hbm, sems.at[1])
-    table = pltpu.make_async_copy(tab_hbm.at[q_ref[0]], tab_ref, sems.at[2, 0])
-    for copy in loads[:1] + [table] + loads[1:]:
+def calibrate_kernel(v_ref, g_ref, cal_ref):
+    for chunk in CHUNKS:
+        calibrate_rows(v_ref, g_ref, cal_ref, *chunk)
+
+
+def power_kernel(count, q_ref, cal_ref, tab_hbm, bank_ref, *refs):
+    out_refs, tot_ref = refs[:count], refs[count]
+    tab_ref, formed, tot_parts, tab_sems = refs[count + 1 :]
+    tables = [
+        pltpu.make_async_copy(tab_hbm.at[q_ref[n]], tab_ref.at[n], tab_sems.at[n]) for n in range(count)
+    ]
+    for copy in tables:
         copy.start()
-    for i in range(len(CHUNKS) + 1):
-        if i < len(CHUNKS):
-            loads[i].wait()
-            calibrate_rows(v_ref, g_ref, cal_ref, *CHUNKS[i])
-            stores[i].start()
-        if i == 0:
-            table.wait()
-        else:
-            form(cal_ref, tab_ref, formed, *CHUNKS[i - 1])
-    filter_power(bank_ref, formed, out_ref, tot_ref)
-    for copy in stores:
-        copy.wait()
-
-
-REST = POL - 1
-
-
-def rest_kernel(q_ref, cal_hbm, tab_hbm, bank_ref, *refs):
-    out_hbms, tot_ref = refs[:REST], refs[REST]
-    cal_ref, tab_ref, formed, out_ref, tot_parts, cal_sems, tab_sems, out_sems = refs[REST + 1 :]
-    loads = row_copies(cal_hbm, cal_ref, cal_sems)
-    tables = [
-        pltpu.make_async_copy(tab_hbm.at[q_ref[n]], tab_ref.at[n], tab_sems.at[n]) for n in range(REST)
-    ]
-    for copy in tables[:1] + loads + tables[1:]:
-        copy.start()
-    stores = []
-    for n in range(REST):
+    for n in range(count):
         tables[n].wait()
-        for i, chunk in enumerate(CHUNKS):
-            if n == 0:
-                loads[i].wait()
+        for chunk in CHUNKS:
             form(cal_ref, tab_ref.at[n], formed.at[n], *chunk)
-        filter_power(bank_ref, formed.at[n], out_ref.at[n], tot_parts.at[n])
-        stores.append(pltpu.make_async_copy(out_ref.at[n], out_hbms[n], out_sems.at[n]))
-        stores[-1].start()
-    tot_ref[...] = tot_parts[0] + tot_parts[1] + tot_parts[2]
-    for copy in stores:
-        copy.wait()
-
-
+        filter_power(bank_ref, formed.at[n], out_refs[n], tot_parts.at[n])
+    total = tot_parts[0]
+    for n in range(1, count):
+        total = total + tot_parts[n]
+    tot_ref[...] = total
+
+
+BRIEF = pl.CostEstimate(flops=100_000_000, bytes_accessed=10_000, transcendentals=0)
 POWER = jax.ShapeDtypeStruct((UP * FR, QUARTER), jnp.bfloat16)
 TOTAL = jax.ShapeDtypeStruct((UP, 128), jnp.float32)
-def lead_power(index, voltages, gains, tables, bank):
+def calibrate(voltages, gains):
     flat = voltages.reshape(TS, 2, TILES, 128).transpose(0, 2, 1, 3).reshape(TS * KINDS, 128)
     return pl.pallas_call(
-        lead_kernel,
-        in_specs=[SMEM, HBM, VMEM, HBM, VMEM],
-        out_specs=[VMEM, VMEM, HBM],
-        out_shape=[POWER, TOTAL, jax.ShapeDtypeStruct((TS, 2 * FEEDS), jnp.bfloat16)],
+        calibrate_kernel,
+        in_specs=[VMEM, VMEM],
+        out_specs=VMEM,
+        out_shape=jax.ShapeDtypeStruct((TS, 2 * FEEDS), jnp.bfloat16),
+        compiler_params=PARAMS,
+        name="calibrate",
+    )(flat, gains)
+
+
+def quarter_powers(indices, calibrated, tables, bank):
+    count = len(indices)
+    return pl.pallas_call(
+        functools.partial(power_kernel, count),
+        in_specs=[SMEM, VMEM, HBM, VMEM],
+        out_specs=[VMEM] * (count + 1),
+        out_shape=[POWER] * count + [TOTAL],
         scratch_shapes=[
-            pltpu.VMEM((TS * KINDS, 128), jnp.bfloat16),
-            pltpu.VMEM((2 * FEEDS, 2 * QUARTER), jnp.bfloat16),
-            pltpu.VMEM((TS, 2 * FEEDS), jnp.bfloat16),
-            pltpu.VMEM((TS, 2 * QUARTER), jnp.bfloat16),
-            pltpu.SemaphoreType.DMA((3, len(CHUNKS))),
+            pltpu.VMEM((count, 2 * FEEDS, 2 * QUARTER), jnp.bfloat16),
+            pltpu.VMEM((count, TS, 2 * QUARTER), jnp.bfloat16),
+            pltpu.VMEM((count, UP, 128), jnp.float32),
+            pltpu.SemaphoreType.DMA((count,)),
         ],
         compiler_params=WHOLE,
-        cost_estimate=pl.CostEstimate(flops=3_000_000_000, bytes_accessed=8_000_000, transcendentals=0),
-        name="lead_power",
-    )(index.reshape(1), flat, gains, tables, bank)
-
-
-def rest_powers(indices, calibrated, tables, bank):
-    return pl.pallas_call(
-        rest_kernel,
-        in_specs=[SMEM, HBM, HBM, VMEM],
-        out_specs=[HBM] * REST + [VMEM],
-        out_shape=[POWER] * REST + [TOTAL],
-        scratch_shapes=[
-            pltpu.VMEM((TS, 2 * FEEDS), jnp.bfloat16),
-            pltpu.VMEM((REST, 2 * FEEDS, 2 * QUARTER), jnp.bfloat16),
-            pltpu.VMEM((REST, TS, 2 * QUARTER), jnp.bfloat16),
-            pltpu.VMEM((REST, UP * FR, QUARTER), jnp.bfloat16),
-            pltpu.VMEM((REST, UP, 128), jnp.float32),
-            pltpu.SemaphoreType.DMA((len(CHUNKS),)),
-            pltpu.SemaphoreType.DMA((REST,)),
-            pltpu.SemaphoreType.DMA((REST,)),
-        ],
-        compiler_params=WHOLE,
-        cost_estimate=pl.CostEstimate(flops=9_000_000_000, bytes_accessed=8_000_000, transcendentals=0),
-        name="rest_powers",
+        cost_estimate=BRIEF,
+        name="quarter_powers",
     )(jnp.stack(indices), calibrated, tables, bank)
 
 
@@ -384,11 +341,14 @@
     def send(power, ahead):
         return lax.ppermute(power, "pol", [(i, (i + ahead) % POL) for i in range(POL)])
 
-    far, far_total, calibrated = lead_power(index[2], voltages[0, 0], gains[0, 0], tables, bank)
-    far = send(far, 2)
-    right, left, own, rest_total = rest_powers([index[1], index[3], index[0]], calibrated, tables, bank)
-    parts = [far, send(right, 1), send(left, 3), own]
-    normed = normalize(lax.psum(far_total + rest_total, "pol"), parts)
+    calibrated = calibrate(voltages[0, 0], gains[0, 0])
+    parts, totals = [], 0.0
+    for ahead in (2, 1, 3):
+        power, total = quarter_powers([index[ahead]], calibrated, tables, bank)
+        parts.append(send(power, ahead))
+        totals = totals + total
+    own, total = quarter_powers([index[0]], calibrated, tables, bank)
+    normed = normalize(lax.psum(totals + total, "pol"), parts + [own])
     alike = [[CORES * chip + c for chip in range(CHIPS)] for c in range(CORES)]
     turned = lax.all_to_all(
         normed.reshape(CHIPS, CORES, PAIR * UP * FR), "freq", 0, 0, tiled=True, axis_index_groups=alike

time: 111 us -> 102 us (0.919)
  blocking collectives: 39 us -> 23.6 us
  starting transfers between devices: 27.2 us -> 30.6 us
  local copies, waits for them, and re-layouts: 2.86 us -> 6.14 us
  other arithmetic: 2.83 us -> 1.46 us
    psum x1, blocking collectives: 22.2 us -> 9.36 us  [on_device(): normed = normalize(lax.psum(totals + total, 'pol'), parts + [own])]
    unnamed x14 -> x18, local copies, waits for them, and re-layouts: 1.09 us -> 4.38 us
    all_to_all x1, blocking collectives: 16.8 us -> 14.3 us  [on_device(): lax.all_to_all(out, ('freq', 'pol'), 0, 0, tiled=True, axis_index_groups=...]
    all_to_all x1, starting transfers between devices: 16.4 us -> 18.7 us  [on_device(): lax.all_to_all(normed.reshape(CHIPS, CORES, PAIR * UP * FR), 'freq', 0, 0...]
    pallas_call x1, Pallas kernels: 0.54 us -> 1.96 us  [normalize(): pl.pallas_call(normalize_kernel, in_specs=[VMEM] * (1 + POL), out_specs=V...]
    ppermute x3, starting transfers between devices: 10.8 us -> 12 us  [send(): lax.ppermute(power, 'pol', [(i, (i + ahead) % POL) for i in range(POL)])]
    pallas_call x2 -> x5, Pallas kernels: 21.1 us -> 20.1 us  [the longest x4 17.9 us: quarter_powers(): pl.pallas_call(functools.partial(power_kernel, count), in_specs=[SMEM, VM...]
  transfers between devices with their start and end apart: 4 -> 4, of which waited for: 1 -> 1; matrix products, arithmetic and copies ran while one was open for 2% -> 1% of each run, Pallas kernels for 0% -> 13%
where the time goes in v3:
time: 102 us
  starting transfers between devices  30.6 us (30%)
  Pallas kernels  25 us (25%)
  blocking collectives  23.6 us (23%)
  waiting for transfers between devices  13.7 us (13%)
  local copies, waits for them, and re-layouts  6.14 us (6%)
  other arithmetic  1.46 us (1%)
    all_to_all x1, starting transfers between devices, on_device(): lax.all_to_all(normed.reshape(CHIPS, CORES, PAIR * UP * FR), 'freq', 0, 0...  18.7 us
    pallas_call x4, Pallas kernels, quarter_powers(): pl.pallas_call(functools.partial(power_kernel, count), in_specs=[SMEM, VM...  17.9 us
    all_to_all x1, blocking collectives, on_device(): lax.all_to_all(out, ('freq', 'pol'), 0, 0, tiled=True, axis_index_groups=...  14.3 us
    all_to_all x1, waiting for transfers between devices, on_device(): lax.all_to_all(normed.reshape(CHIPS, CORES, PAIR * UP * FR), 'freq', 0, 0...  13.7 us
    ppermute x3, starting transfers between devices, send(): lax.ppermute(power, 'pol', [(i, (i + ahead) % POL) for i in range(POL)])  12 us
    psum x1, blocking collectives, on_device(): normed = normalize(lax.psum(totals + total, 'pol'), parts + [own])  9.36 us
    unnamed x18, local copies, waits for them, and re-layouts  4.38 us
    pallas_call x1, Pallas kernels, dedisperse(): pl.pallas_call(dedisperse_kernel, in_specs=[SMEM, VMEM, VMEM, VMEM, VMEM]...  2.93 us
  transfers between devices with their start and end apart: 4, of which 1 were waited for; matrix products, arithmetic and copies ran while one was open for 1% of the time, Pallas kernels for 13%

profile of v3, /device:TPU:1, one launch (start us, length us, event | category | flops | bytes accessed | tf_op | source)
XLA Modules:
  0.0 101.6 jit_solution(3269045232996223908)
XLA Ops:
  0.0 0.0 copy-start.1
  0.0 1.8 %copy-done.1 = bf16[1,1,1392,2,512]{4,3,2,1,0:T(2,128)(2,1)S(1)} copy-done((bf16[1,1,1392,2,512]{4,3,2,1,0:T(2,128)(2,1)S(1)}, bf16[1,1,1392,2,512]{4,3,2,1,0:T(2,128)(2,1)}, u32[]{:S(2)}) %copy-start.1) | copy-done | bytes 2850840
  1.8 0.0 copy-start.6
  1.8 0.7 copy-done.6
  2.5 0.0 copy-start
  2.5 2.2 %calibrate.1.cal_ref = bf16[1392,1024]{1,0:T(8,128)(2,1)S(1)} custom-call(bf16[11136,128]{1,0:T(8,128)(2,1)S(1)} %bitcast.18, f32[2,512]{1,0:T(2,128)S(1)} %bitcast.20), custom_call_target="tpu_custom_call" | custom-call | tf_op jit(solution)/shard_map/calibrate/pallas_call | solution.py:196
  4.7 0.0 copy-done
  4.7 4.6 %quarter_powers.4 = (bf16[1152,256]{1,0:T(8,128)(2,1)}, f32[16,128]{1,0:T(8,128)S(1)}) custom-call(s32[1]{0:T(128)} %bitcast.1.q_ref, bf16[1392,1024]{1,0:T(8,128)(2,1)S(1)} %calibrate.1.cal_ref, bf16[4,1024,512]{2,1,0:T(8,128)(2,1)} %constant.71.clone.tab_hbm, bf16[256,736]{1,0:T(8,128)(2,1)S(1)} %copy-done), custom_call_target="tpu_custom_call" | custom-call | flops 100000000 | bytes 10000 | tf_op jit(solution)/shard_map/quarter_powers/pallas_call | solution.py:208
  9.4 5.5 %collective-permute-start = (bf16[1152,256]{1,0:T(8,128)(2,1)}, bf16[1152,256]{1,0:T(8,128)(2,1)}, u32[]{:S(2)}, u32[]{:S(2)}) collective-permute-start(bf16[1152,256]{1,0:T(8,128)(2,1)} %get-tuple-element.17), channel_id=1, source_target_pairs={{0,2},{1,3},{2,0},{3,1},{4,6},{5,7},{6,4},{7,5},{8,10},{9,11},{10,... | collective-permute-start | bytes 1769480 | tf_op jit(solution)/shard_map/ppermute | solution.py:342
  14.9 4.6 %quarter_powers.5 = (bf16[1152,256]{1,0:T(8,128)(2,1)}, f32[16,128]{1,0:T(8,128)S(1)}) custom-call(s32[1]{0:T(128)} %bitcast.6.q_ref, bf16[1392,1024]{1,0:T(8,128)(2,1)S(1)} %calibrate.1.cal_ref, bf16[4,1024,512]{2,1,0:T(8,128)(2,1)} %constant.71.clone.tab_hbm, bf16[256,736]{1,0:T(8,128)(2,1)S(1)} %copy-done), custom_call_target="tpu_custom_call" | custom-call | flops 100000000 | bytes 10000 | tf_op jit(solution)/shard_map/quarter_powers/pallas_call | solution.py:208
  19.5 2.2 %collective-permute-start.1 = (bf16[1152,256]{1,0:T(8,128)(2,1)}, bf16[1152,256]{1,0:T(8,128)(2,1)}, u32[]{:S(2)}, u32[]{:S(2)}) collective-permute-start(bf16[1152,256]{1,0:T(8,128)(2,1)} %get-tuple-element.18), channel_id=1, source_target_pairs={{0,1},{1,2},{2,3},{3,0},{4,5},{5,6},{6,7},{7,4},{8,9},{9,10},{10,1... | collective-permute-start | bytes 1769480 | tf_op jit(solution)/shard_map/ppermute | solution.py:342
  21.8 4.6 %quarter_powers.6 = (bf16[1152,256]{1,0:T(8,128)(2,1)}, f32[16,128]{1,0:T(8,128)S(1)}) custom-call(s32[1]{0:T(128)} %bitcast.7.q_ref, bf16[1392,1024]{1,0:T(8,128)(2,1)S(1)} %calibrate.1.cal_ref, bf16[4,1024,512]{2,1,0:T(8,128)(2,1)} %constant.71.clone.tab_hbm, bf16[256,736]{1,0:T(8,128)(2,1)S(1)} %copy-done), custom_call_target="tpu_custom_call" | custom-call | flops 100000000 | bytes 10000 | tf_op jit(solution)/shard_map/quarter_powers/pallas_call | solution.py:208
  26.4 4.3 %collective-permute-start.2 = (bf16[1152,256]{1,0:T(8,128)(2,1)}, bf16[1152,256]{1,0:T(8,128)(2,1)}, u32[]{:S(2)}, u32[]{:S(2)}) collective-permute-start(bf16[1152,256]{1,0:T(8,128)(2,1)} %get-tuple-element.19), channel_id=1, source_target_pairs={{0,3},{1,0},{2,1},{3,2},{4,7},{5,4},{6,5},{7,6},{8,11},{9,8},{10,9... | collective-permute-start | bytes 1769480 | tf_op jit(solution)/shard_map/ppermute | solution.py:342
  30.7 4.0 %quarter_powers.7 = (bf16[1152,256]{1,0:T(8,128)(2,1)S(1)}, f32[16,128]{1,0:T(8,128)S(1)}) custom-call(s32[1]{0:T(128)} %bitcast.8.q_ref, bf16[1392,1024]{1,0:T(8,128)(2,1)S(1)} %calibrate.1.cal_ref, bf16[4,1024,512]{2,1,0:T(8,128)(2,1)} %constant.71.clone.tab_hbm, bf16[256,736]{1,0:T(8,128)(2,1)S(1)} %copy-done), custom_call_target="tpu_custom_call" | custom-call | flops 100000000 | bytes 10000 | tf_op jit(solution)/shard_map/quarter_powers/pallas_call | solution.py:208
  34.7 0.0 copy-start.2
  34.7 0.8 copy-done.2
  35.5 0.0 copy-start.7
  35.5 0.0 copy-start.8
  35.5 9.4 %psum.7.tot_ref = f32[16,128]{1,0:T(8,128)S(1)} all-reduce(f32[16,128]{1,0:T(8,128)S(1)} %add_add_fusion), channel_id=1, replica_groups=mesh['freq'=128,'pol'=4] {'pol'}, use_global_device_ids=true, to_apply=%region_1.2 | all-reduce | flops 2048 | bytes 16384 | tf_op jit(solution)/shard_map/psum | solution.py:351
  44.8 0.0 collective-permute-done.a_ref
  44.9 0.0 collective-permute-done.1.b_ref
  44.9 0.0 collective-permute-done.2.c_ref
  44.9 0.0 copy-start.3
  44.9 1.1 %copy-done.3 = bf16[1152,256]{1,0:T(8,128)(2,1)S(1)} copy-done((bf16[1152,256]{1,0:T(8,128)(2,1)S(1)}, bf16[1152,256]{1,0:T(8,128)(2,1)}, u32[]{:S(2)}) %copy-start.3) | copy-done | bytes 589848
  45.9 2.0 %normalize.1 = bf16[128,2304]{1,0:T(8,128)(2,1)S(1)} custom-call(f32[16,128]{1,0:T(8,128)S(1)} %psum.7.tot_ref, bf16[1152,256]{1,0:T(8,128)(2,1)} %collective-permute-done.a_ref, bf16[1152,256]{1,0:T(8,128)(2,1)} %collective-permute-done.1.b_ref, bf16[1152,256]{1,0:T(8,128)(2,1)} %collective-permute-done.2.c_ref, bf16[1152,256]{1,0:T(8,128)(2,1)S(1)} %copy-done.3), custom_call_target="tpu_custom_call" | custom-call | tf_op jit(solution)/shard_map/normalize/pallas_call | solution.py:244
  47.9 0.0 copy-start.4
  47.9 0.0 copy-start.5
  47.9 1.0 %reshape.77 = bf16[64,2,2304]{2,1,0:T(2,128)(2,1)} reshape(bf16[128,2304]{1,0:T(8,128)(2,1)S(1)} %normalize.1) | data formatting | bytes 1179648 | tf_op jit(solution)/shard_map/reshape | solution.py:354
  49.0 18.7 %all-to-all-start = ((bf16[64,2,2304]{2,1,0:T(2,128)(2,1)}), bf16[64,2,2304]{2,1,0:T(2,128)(2,1)S(1)}, u32[]{:S(2)}, u32[]{:S(2)}) async-start(bf16[64,2,2304]{2,1,0:T(2,128)(2,1)} %reshape.77), calls=%async_computation | async-start | bytes 1179648 | tf_op jit(solution)/shard_map/all_to_all | solution.py:353
  67.7 0.0 copy-done.7
  67.7 0.0 copy-done.8
  67.7 0.6 compare_select_fusion
  68.3 0.1 reshape.79
  68.5 0.1 copy.16
  68.6 0.1 reshape.80
  68.6 0.1 copy.17
  68.8 0.1 copy.18
  69.6 0.1 iota_compare_fusion
  69.6 0.1 and_convert_fusion
  69.8 13.7 %all-to-all-done = bf16[64,2,2304]{2,1,0:T(2,128)(2,1)S(1)} async-done(((bf16[64,2,2304]{2,1,0:T(2,128)(2,1)}), bf16[64,2,2304]{2,1,0:T(2,128)(2,1)S(1)}, u32[]{:S(2)}, u32[]{:S(2)}) %all-to-all-start) | async-done | bytes 589856 | tf_op jit(solution)/shard_map/all_to_all | solution.py:353
  83.5 0.2 reshape.78.x_ref
  83.7 0.0 copy-done.4
  83.7 0.0 copy-done.5
  83.7 2.9 %dedisperse.1 = f32[8,2,24,128]{3,2,1,0:T(8,128)S(1)} custom-call(f32[1,1]{1,0:T(1,128)} %bitcast.scale_ref, bf16[128,2304]{1,0:T(8,128)(2,1)S(1)} %reshape.78.x_ref, bf16[896,256]{1,0:T(8,128)(2,1)S(1)} %bitcast.19, bf16[1152,128]{1,0:T(8,128)(2,1)S(1)} %copy-done.5, bf16[128,1736]{1,0:T(8,128)(2,1)S(1)} %copy-done.4), custom_call_target="tpu_custom_call" | custom-call | tf_op jit(solution)/shard_map/dedisperse/pallas_call | solution.py:309
  86.6 14.3 %all_to_all.10 = f32[8,2,24,128]{3,2,1,0:T(8,128)S(1)} all-to-all(f32[8,2,24,128]{3,2,1,0:T(8,128)S(1)} %dedisperse.1), channel_id=1, replica_groups={{0,1,2,3,4,5,6,7},{8,9,10,11,12,13,14,15},{16,17,18,19,20,21,22,23},{24..., dimensions={0} | all-to-all | bytes 393216 | tf_op jit(solution)/shard_map/all_to_all | solution.py:361
  100.9 0.7 slice_add_fusion
  (5 shorter events, 0.1 us)
Async XLA Ops:
  0.0 1.8 %copy-start.1 = (bf16[1,1,1392,2,512]{4,3,2,1,0:T(2,128)(2,1)S(1)}, bf16[1,1,1392,2,512]{4,3,2,1,0:T(2,128)(2,1)}, u32[]{:S(2)}) copy-start(bf16[1,1,1392,2,512]{4,3,2,1,0:T(2,128)(2,1)} %param.8) | copy-start | bytes 8552452
  1.8 0.7 copy-start.6
  2.5 2.2 %copy-start = (bf16[256,736]{1,0:T(8,128)(2,1)S(1)}, bf16[256,736]{1,0:T(8,128)(2,1)}, u32[]{:S(2)}) copy-start(bf16[256,736]{1,0:T(8,128)(2,1)} %constant.72.clone.bank_ref) | copy-start | bytes 1130500
  9.4 35.5 %collective-permute-start = (bf16[1152,256]{1,0:T(8,128)(2,1)}, bf16[1152,256]{1,0:T(8,128)(2,1)}, u32[]{:S(2)}, u32[]{:S(2)}) collective-permute-start(bf16[1152,256]{1,0:T(8,128)(2,1)} %get-tuple-element.17), channel_id=1, source_target_pairs={{0,2},{1,3},{2,0},{3,1},{4,6},{5,7},{6,4},{7,5},{8,10},{9,11},{10,... | collective-permute-start | bytes 1769480 | tf_op jit(solution)/shard_map/ppermute | solution.py:342
  19.5 25.3 %collective-permute-start.1 = (bf16[1152,256]{1,0:T(8,128)(2,1)}, bf16[1152,256]{1,0:T(8,128)(2,1)}, u32[]{:S(2)}, u32[]{:S(2)}) collective-permute-start(bf16[1152,256]{1,0:T(8,128)(2,1)} %get-tuple-element.18), channel_id=1, source_target_pairs={{0,1},{1,2},{2,3},{3,0},{4,5},{5,6},{6,7},{7,4},{8,9},{9,10},{10,1... | collective-permute-start | bytes 1769480 | tf_op jit(solution)/shard_map/ppermute | solution.py:342
  26.4 18.5 %collective-permute-start.2 = (bf16[1152,256]{1,0:T(8,128)(2,1)}, bf16[1152,256]{1,0:T(8,128)(2,1)}, u32[]{:S(2)}, u32[]{:S(2)}) collective-permute-start(bf16[1152,256]{1,0:T(8,128)(2,1)} %get-tuple-element.19), channel_id=1, source_target_pairs={{0,3},{1,0},{2,1},{3,2},{4,7},{5,4},{6,5},{7,6},{8,11},{9,8},{10,9... | collective-permute-start | bytes 1769480 | tf_op jit(solution)/shard_map/ppermute | solution.py:342
  34.7 0.8 copy-start.2
  35.5 32.2 %copy-start.7 = (s32[2048]{0:T(1024)S(1)}, s32[2048]{0:T(1024)}, u32[]{:S(2)}) copy-start(s32[2048]{0:T(1024)} %param.10) | copy-start | bytes 24580
  35.5 32.2 %copy-start.8 = (s32[2048]{0:T(1024)S(1)}, s32[2048]{0:T(1024)}, u32[]{:S(2)}) copy-start(s32[2048]{0:T(1024)} %param.11) | copy-start | bytes 24580
  44.9 1.1 %copy-start.3 = (bf16[1152,256]{1,0:T(8,128)(2,1)S(1)}, bf16[1152,256]{1,0:T(8,128)(2,1)}, u32[]{:S(2)}) copy-start(bf16[1152,256]{1,0:T(8,128)(2,1)} %copy-done.2) | copy-start | bytes 1769476
  47.9 35.8 %copy-start.4 = (bf16[128,1736]{1,0:T(8,128)(2,1)S(1)}, bf16[128,1736]{1,0:T(8,128)(2,1)}, u32[]{:S(2)}) copy-start(bf16[128,1736]{1,0:T(8,128)(2,1)} %constant.74.clone.trial_ref) | copy-start | bytes 1333252
  47.9 35.8 %copy-start.5 = (bf16[1152,128]{1,0:T(8,128)(2,1)S(1)}, bf16[1152,128]{1,0:T(8,128)(2,1)}, u32[]{:S(2)}) copy-start(bf16[1152,128]{1,0:T(8,128)(2,1)} %constant.73.clone.fold_ref) | copy-start | bytes 884740
  49.0 34.5 %all-to-all-start = ((bf16[64,2,2304]{2,1,0:T(2,128)(2,1)}), bf16[64,2,2304]{2,1,0:T(2,128)(2,1)S(1)}, u32[]{:S(2)}, u32[]{:S(2)}) async-start(bf16[64,2,2304]{2,1,0:T(2,128)(2,1)} %reshape.77), calls=%async_computation | async-start | bytes 1179648 | tf_op jit(solution)/shard_map/all_to_all | solution.py:353

commit v4 on v3

--- a/solution.py
+++ b/solution.py
@@ -30,7 +30,7 @@
 SLOTS = 56
 TILES = FEEDS // 128
 KINDS = 2 * TILES
-CHUNKS = ((0, 464), (464, 464), (928, 464))
+CHUNKS = ((0, 368), (368, 512), (880, 512))
 CORES = 2
 CHIPS = FREQ // CORES
 HELD = CORES * PAIR
@@ -164,8 +164,17 @@
         tot_ref[u : u + 1, :] = jnp.broadcast_to(jnp.sum(part, keepdims=True), (1, 128))
 
 
-def calibrate_kernel(v_ref, g_ref, cal_ref):
-    for chunk in CHUNKS:
+def calibrate_kernel(v_hbm, g_hbm, cal_ref, v_ref, g_ref, sems):
+    loads = []
+    for i, (start, size) in enumerate(CHUNKS):
+        rows = pl.ds(start * KINDS, size * KINDS)
+        loads.append(pltpu.make_async_copy(v_hbm.at[rows, :], v_ref.at[rows, :], sems.at[i]))
+    gains = pltpu.make_async_copy(g_hbm, g_ref, sems.at[len(CHUNKS)])
+    for copy in [gains] + loads:
+        copy.start()
+    gains.wait()
+    for copy, chunk in zip(loads, CHUNKS):
+        copy.wait()
         calibrate_rows(v_ref, g_ref, cal_ref, *chunk)
 
 
@@ -195,10 +204,15 @@
     flat = voltages.reshape(TS, 2, TILES, 128).transpose(0, 2, 1, 3).reshape(TS * KINDS, 128)
     return pl.pallas_call(
         calibrate_kernel,
-        in_specs=[VMEM, VMEM],
+        in_specs=[HBM, HBM],
         out_specs=VMEM,
         out_shape=jax.ShapeDtypeStruct((TS, 2 * FEEDS), jnp.bfloat16),
-        compiler_params=PARAMS,
+        scratch_shapes=[
+            pltpu.VMEM((TS * KINDS, 128), jnp.bfloat16),
+            pltpu.VMEM((2, FEEDS), jnp.float32),
+            pltpu.SemaphoreType.DMA((len(CHUNKS) + 1,)),
+        ],
+        compiler_params=pltpu.CompilerParams(vmem_limit_bytes=50 * 1024 * 1024),
         name="calibrate",
     )(flat, gains)
 
@@ -247,7 +261,7 @@
         out_specs=VMEM,
         out_shape=jax.ShapeDtypeStruct((FREQ, PAIR * UP * FR), jnp.bfloat16),
         scratch_shapes=[pltpu.VMEM((ROWS, 128), jnp.float32)],
-        compiler_params=PARAMS,
+        compiler_params=pltpu.CompilerParams(vmem_limit_bytes=60 * 1024 * 1024),
         name="normalize",
     )(totals, *parts)
 

time: 102 us -> 104 us (1.020)
  Pallas kernels: 25 us -> 27.3 us
  local copies, waits for them, and re-layouts: 6.14 us -> 4.92 us
    unnamed x18 -> x14, local copies, waits for them, and re-layouts: 4.38 us -> 1.51 us
    reshape x1, local copies, waits for them, and re-layouts: 1.04 us -> 2.69 us  [on_device(): normed.reshape(CHIPS, CORES, PAIR * UP * FR)]
    pallas_call x1, Pallas kernels: 2.19 us -> 3.36 us  [calibrate(): pl.pallas_call(calibrate_kernel, in_specs=[HBM, HBM], out_specs=VMEM, out...]
where the time goes in v4:
time: 104 us; the launch traced here: 103 us
  starting transfers between devices  30.6 us (29%)
  Pallas kernels  27.3 us (26%)
  blocking collectives  24 us (23%)
  waiting for transfers between devices  13.7 us (13%)
  local copies, waits for them, and re-layouts  4.92 us (5%)
  other arithmetic  1.46 us (1%)
    all_to_all x1, starting transfers between devices, on_device(): lax.all_to_all(normed.reshape(CHIPS, CORES, PAIR * UP * FR), 'freq', 0, 0...  18.7 us
    pallas_call x4, Pallas kernels, quarter_powers(): pl.pallas_call(functools.partial(power_kernel, count), in_specs=[SMEM, VM...  18 us
    all_to_all x1, blocking collectives, on_device(): lax.all_to_all(out, ('freq', 'pol'), 0, 0, tiled=True, axis_index_groups=...  14.3 us
    all_to_all x1, waiting for transfers between devices, on_device(): lax.all_to_all(normed.reshape(CHIPS, CORES, PAIR * UP * FR), 'freq', 0, 0...  13.7 us
    ppermute x3, starting transfers between devices, send(): lax.ppermute(power, 'pol', [(i, (i + ahead) % POL) for i in range(POL)])  12 us
    psum x1, blocking collectives, on_device(): normed = normalize(lax.psum(totals + total, 'pol'), parts + [own])  9.72 us
    pallas_call x1, Pallas kernels, calibrate(): pl.pallas_call(calibrate_kernel, in_specs=[HBM, HBM], out_specs=VMEM, out...  3.36 us
    pallas_call x1, Pallas kernels, normalize(): pl.pallas_call(normalize_kernel, in_specs=[VMEM] * (1 + POL), out_specs=V...  3 us
  transfers between devices with their start and end apart: 4, of which 1 were waited for; matrix products, arithmetic and copies ran while one was open for 1% of the time, Pallas kernels for 13%

profile of v4, /device:TPU:1, one launch (start us, length us, event | category | flops | bytes accessed | tf_op | source)
XLA Modules:
  0.0 103.0 jit_solution(6016447532171354341)
XLA Ops:
  0.0 0.0 copy-start.4
  0.0 0.7 copy-done.4
  0.7 0.0 copy-start
  0.7 3.4 %calibrate.1.cal_ref = bf16[1392,1024]{1,0:T(8,128)(2,1)S(1)} custom-call(bf16[11136,128]{1,0:T(8,128)(2,1)} %bitcast.20, f32[2,512]{1,0:T(2,128)S(1)} %bitcast.19), custom_call_target="tpu_custom_call" | custom-call | tf_op jit(solution)/shard_map/calibrate/pallas_call | solution.py:205
  4.1 0.0 copy-done
  4.1 4.7 %quarter_powers.4 = (bf16[1152,256]{1,0:T(8,128)(2,1)}, f32[16,128]{1,0:T(8,128)S(1)}) custom-call(s32[1]{0:T(128)} %bitcast.1.q_ref, bf16[1392,1024]{1,0:T(8,128)(2,1)S(1)} %calibrate.1.cal_ref, bf16[4,1024,512]{2,1,0:T(8,128)(2,1)} %constant.71.clone.tab_hbm, bf16[256,736]{1,0:T(8,128)(2,1)S(1)} %copy-done), custom_call_target="tpu_custom_call" | custom-call | flops 100000000 | bytes 10000 | tf_op jit(solution)/shard_map/quarter_powers/pallas_call | solution.py:222
  8.8 5.5 %collective-permute-start = (bf16[1152,256]{1,0:T(8,128)(2,1)}, bf16[1152,256]{1,0:T(8,128)(2,1)}, u32[]{:S(2)}, u32[]{:S(2)}) collective-permute-start(bf16[1152,256]{1,0:T(8,128)(2,1)} %get-tuple-element.17), channel_id=1, source_target_pairs={{0,2},{1,3},{2,0},{3,1},{4,6},{5,7},{6,4},{7,5},{8,10},{9,11},{10,... | collective-permute-start | bytes 1769480 | tf_op jit(solution)/shard_map/ppermute | solution.py:356
  14.3 4.7 %quarter_powers.5 = (bf16[1152,256]{1,0:T(8,128)(2,1)}, f32[16,128]{1,0:T(8,128)S(1)}) custom-call(s32[1]{0:T(128)} %bitcast.6.q_ref, bf16[1392,1024]{1,0:T(8,128)(2,1)S(1)} %calibrate.1.cal_ref, bf16[4,1024,512]{2,1,0:T(8,128)(2,1)} %constant.71.clone.tab_hbm, bf16[256,736]{1,0:T(8,128)(2,1)S(1)} %copy-done), custom_call_target="tpu_custom_call" | custom-call | flops 100000000 | bytes 10000 | tf_op jit(solution)/shard_map/quarter_powers/pallas_call | solution.py:222
  18.9 2.2 %collective-permute-start.1 = (bf16[1152,256]{1,0:T(8,128)(2,1)}, bf16[1152,256]{1,0:T(8,128)(2,1)}, u32[]{:S(2)}, u32[]{:S(2)}) collective-permute-start(bf16[1152,256]{1,0:T(8,128)(2,1)} %get-tuple-element.18), channel_id=1, source_target_pairs={{0,1},{1,2},{2,3},{3,0},{4,5},{5,6},{6,7},{7,4},{8,9},{9,10},{10,1... | collective-permute-start | bytes 1769480 | tf_op jit(solution)/shard_map/ppermute | solution.py:356
  21.2 4.7 %quarter_powers.6 = (bf16[1152,256]{1,0:T(8,128)(2,1)}, f32[16,128]{1,0:T(8,128)S(1)}) custom-call(s32[1]{0:T(128)} %bitcast.7.q_ref, bf16[1392,1024]{1,0:T(8,128)(2,1)S(1)} %calibrate.1.cal_ref, bf16[4,1024,512]{2,1,0:T(8,128)(2,1)} %constant.71.clone.tab_hbm, bf16[256,736]{1,0:T(8,128)(2,1)S(1)} %copy-done), custom_call_target="tpu_custom_call" | custom-call | flops 100000000 | bytes 10000 | tf_op jit(solution)/shard_map/quarter_powers/pallas_call | solution.py:222
  25.9 4.3 %collective-permute-start.2 = (bf16[1152,256]{1,0:T(8,128)(2,1)}, bf16[1152,256]{1,0:T(8,128)(2,1)}, u32[]{:S(2)}, u32[]{:S(2)}) collective-permute-start(bf16[1152,256]{1,0:T(8,128)(2,1)} %get-tuple-element.19), channel_id=1, source_target_pairs={{0,3},{1,0},{2,1},{3,2},{4,7},{5,4},{6,5},{7,6},{8,11},{9,8},{10,9... | collective-permute-start | bytes 1769480 | tf_op jit(solution)/shard_map/ppermute | solution.py:356
  30.1 4.0 %quarter_powers.7 = (bf16[1152,256]{1,0:T(8,128)(2,1)S(1)}, f32[16,128]{1,0:T(8,128)S(1)}) custom-call(s32[1]{0:T(128)} %bitcast.8.q_ref, bf16[1392,1024]{1,0:T(8,128)(2,1)S(1)} %calibrate.1.cal_ref, bf16[4,1024,512]{2,1,0:T(8,128)(2,1)} %constant.71.clone.tab_hbm, bf16[256,736]{1,0:T(8,128)(2,1)S(1)} %copy-done), custom_call_target="tpu_custom_call" | custom-call | flops 100000000 | bytes 10000 | tf_op jit(solution)/shard_map/quarter_powers/pallas_call | solution.py:222
  34.2 0.0 copy-start.1
  34.2 0.8 copy-done.1
  35.0 0.0 copy-start.5
  35.0 0.0 copy-start.6
  35.0 9.7 %psum.7.tot_ref = f32[16,128]{1,0:T(8,128)} all-reduce(f32[16,128]{1,0:T(8,128)S(1)} %add_add_fusion), channel_id=1, replica_groups=mesh['freq'=128,'pol'=4] {'pol'}, use_global_device_ids=true, to_apply=%region_1.2 | all-reduce | flops 2048 | bytes 16384 | tf_op jit(solution)/shard_map/psum | solution.py:365
  44.7 0.0 collective-permute-done.a_ref
  44.7 0.0 collective-permute-done.1.b_ref
  44.7 0.0 collective-permute-done.2.c_ref
  44.7 3.0 %normalize.1 = bf16[128,2304]{1,0:T(8,128)(2,1)} custom-call(f32[16,128]{1,0:T(8,128)} %psum.7.tot_ref, bf16[1152,256]{1,0:T(8,128)(2,1)} %collective-permute-done.a_ref, bf16[1152,256]{1,0:T(8,128)(2,1)} %collective-permute-done.1.b_ref, bf16[1152,256]{1,0:T(8,128)(2,1)} %collective-permute-done.2.c_ref, bf16[1152,256]{1,0:T(8,128)(2,1)} %copy-done.1), custom_call_target="tpu_custom_call" | custom-call | tf_op jit(solution)/shard_map/normalize/pallas_call | solution.py:258
  47.7 0.0 copy-start.2
  47.7 0.0 copy-start.3
  47.7 2.7 %reshape.77 = bf16[64,2,2304]{2,1,0:T(2,128)(2,1)} reshape(bf16[128,2304]{1,0:T(8,128)(2,1)} %normalize.1) | data formatting | bytes 1179648 | tf_op jit(solution)/shard_map/reshape | solution.py:368
  50.4 18.7 %all-to-all-start = ((bf16[64,2,2304]{2,1,0:T(2,128)(2,1)}), bf16[64,2,2304]{2,1,0:T(2,128)(2,1)S(1)}, u32[]{:S(2)}, u32[]{:S(2)}) async-start(bf16[64,2,2304]{2,1,0:T(2,128)(2,1)} %reshape.77), calls=%async_computation | async-start | bytes 1179648 | tf_op jit(solution)/shard_map/all_to_all | solution.py:367
  69.1 0.0 copy-done.5
  69.1 0.0 copy-done.6
  69.1 0.6 compare_select_fusion
  69.7 0.1 reshape.79
  69.9 0.1 copy.16
  70.0 0.1 reshape.80
  70.1 0.1 copy.17
  70.2 0.1 copy.18
  71.0 0.1 iota_compare_fusion
  71.1 0.1 and_convert_fusion
  71.2 13.7 %all-to-all-done = bf16[64,2,2304]{2,1,0:T(2,128)(2,1)S(1)} async-done(((bf16[64,2,2304]{2,1,0:T(2,128)(2,1)}), bf16[64,2,2304]{2,1,0:T(2,128)(2,1)S(1)}, u32[]{:S(2)}, u32[]{:S(2)}) %all-to-all-start) | async-done | bytes 589856 | tf_op jit(solution)/shard_map/all_to_all | solution.py:367
  84.9 0.2 reshape.78.x_ref
  85.1 0.0 copy-done.2
  85.1 0.0 copy-done.3
  85.1 2.9 %dedisperse.1 = f32[8,2,24,128]{3,2,1,0:T(8,128)S(1)} custom-call(f32[1,1]{1,0:T(1,128)} %bitcast.scale_ref, bf16[128,2304]{1,0:T(8,128)(2,1)S(1)} %reshape.78.x_ref, bf16[896,256]{1,0:T(8,128)(2,1)S(1)} %bitcast.18, bf16[1152,128]{1,0:T(8,128)(2,1)S(1)} %copy-done.3, bf16[128,1736]{1,0:T(8,128)(2,1)S(1)} %copy-done.2), custom_call_target="tpu_custom_call" | custom-call | tf_op jit(solution)/shard_map/dedisperse/pallas_call | solution.py:323
  88.1 14.3 %all_to_all.10 = f32[8,2,24,128]{3,2,1,0:T(8,128)S(1)} all-to-all(f32[8,2,24,128]{3,2,1,0:T(8,128)S(1)} %dedisperse.1), channel_id=1, replica_groups={{0,1,2,3,4,5,6,7},{8,9,10,11,12,13,14,15},{16,17,18,19,20,21,22,23},{24..., dimensions={0} | all-to-all | bytes 393216 | tf_op jit(solution)/shard_map/all_to_all | solution.py:375
  102.3 0.7 slice_add_fusion
  (5 shorter events, 0.1 us)
Async XLA Ops:
  0.0 0.7 copy-start.4
  0.7 3.4 %copy-start = (bf16[256,736]{1,0:T(8,128)(2,1)S(1)}, bf16[256,736]{1,0:T(8,128)(2,1)}, u32[]{:S(2)}) copy-start(bf16[256,736]{1,0:T(8,128)(2,1)} %constant.72.clone.bank_ref) | copy-start | bytes 1130500
  8.8 35.9 %collective-permute-start = (bf16[1152,256]{1,0:T(8,128)(2,1)}, bf16[1152,256]{1,0:T(8,128)(2,1)}, u32[]{:S(2)}, u32[]{:S(2)}) collective-permute-start(bf16[1152,256]{1,0:T(8,128)(2,1)} %get-tuple-element.17), channel_id=1, source_target_pairs={{0,2},{1,3},{2,0},{3,1},{4,6},{5,7},{6,4},{7,5},{8,10},{9,11},{10,... | collective-permute-start | bytes 1769480 | tf_op jit(solution)/shard_map/ppermute | solution.py:356
  18.9 25.8 %collective-permute-start.1 = (bf16[1152,256]{1,0:T(8,128)(2,1)}, bf16[1152,256]{1,0:T(8,128)(2,1)}, u32[]{:S(2)}, u32[]{:S(2)}) collective-permute-start(bf16[1152,256]{1,0:T(8,128)(2,1)} %get-tuple-element.18), channel_id=1, source_target_pairs={{0,1},{1,2},{2,3},{3,0},{4,5},{5,6},{6,7},{7,4},{8,9},{9,10},{10,1... | collective-permute-start | bytes 1769480 | tf_op jit(solution)/shard_map/ppermute | solution.py:356
  25.9 18.9 %collective-permute-start.2 = (bf16[1152,256]{1,0:T(8,128)(2,1)}, bf16[1152,256]{1,0:T(8,128)(2,1)}, u32[]{:S(2)}, u32[]{:S(2)}) collective-permute-start(bf16[1152,256]{1,0:T(8,128)(2,1)} %get-tuple-element.19), channel_id=1, source_target_pairs={{0,3},{1,0},{2,1},{3,2},{4,7},{5,4},{6,5},{7,6},{8,11},{9,8},{10,9... | collective-permute-start | bytes 1769480 | tf_op jit(solution)/shard_map/ppermute | solution.py:356
  34.2 0.8 copy-start.1
  35.0 34.1 %copy-start.5 = (s32[2048]{0:T(1024)S(1)}, s32[2048]{0:T(1024)}, u32[]{:S(2)}) copy-start(s32[2048]{0:T(1024)} %param.10) | copy-start | bytes 24580
  35.0 34.1 %copy-start.6 = (s32[2048]{0:T(1024)S(1)}, s32[2048]{0:T(1024)}, u32[]{:S(2)}) copy-start(s32[2048]{0:T(1024)} %param.11) | copy-start | bytes 24580
  47.7 37.4 %copy-start.2 = (bf16[128,1736]{1,0:T(8,128)(2,1)S(1)}, bf16[128,1736]{1,0:T(8,128)(2,1)}, u32[]{:S(2)}) copy-start(bf16[128,1736]{1,0:T(8,128)(2,1)} %constant.74.clone.trial_ref) | copy-start | bytes 1333252
  47.7 37.4 %copy-start.3 = (bf16[1152,128]{1,0:T(8,128)(2,1)S(1)}, bf16[1152,128]{1,0:T(8,128)(2,1)}, u32[]{:S(2)}) copy-start(bf16[1152,128]{1,0:T(8,128)(2,1)} %constant.73.clone.fold_ref) | copy-start | bytes 884740
  50.4 34.5 %all-to-all-start = ((bf16[64,2,2304]{2,1,0:T(2,128)(2,1)}), bf16[64,2,2304]{2,1,0:T(2,128)(2,1)S(1)}, u32[]{:S(2)}, u32[]{:S(2)}) async-start(bf16[64,2,2304]{2,1,0:T(2,128)(2,1)} %reshape.77), calls=%async_computation | async-start | bytes 1179648 | tf_op jit(solution)/shard_map/all_to_all | solution.py:367

commit v5 on v3

--- a/solution.py
+++ b/solution.py
@@ -164,62 +164,54 @@
         tot_ref[u : u + 1, :] = jnp.broadcast_to(jnp.sum(part, keepdims=True), (1, 128))
 
 
-def calibrate_kernel(v_ref, g_ref, cal_ref):
-    for chunk in CHUNKS:
-        calibrate_rows(v_ref, g_ref, cal_ref, *chunk)
-
-
-def power_kernel(count, q_ref, cal_ref, tab_hbm, bank_ref, *refs):
-    out_refs, tot_ref = refs[:count], refs[count]
-    tab_ref, formed, tot_parts, tab_sems = refs[count + 1 :]
+def calibrate_kernel(q_ref, v_ref, g_ref, tab_hbm, cal_ref, tab_ref, tab_sems):
     tables = [
-        pltpu.make_async_copy(tab_hbm.at[q_ref[n]], tab_ref.at[n], tab_sems.at[n]) for n in range(count)
+        pltpu.make_async_copy(tab_hbm.at[q_ref[n]], tab_ref.at[n], tab_sems.at[n]) for n in range(POL)
     ]
     for copy in tables:
         copy.start()
-    for n in range(count):
-        tables[n].wait()
-        for chunk in CHUNKS:
-            form(cal_ref, tab_ref.at[n], formed.at[n], *chunk)
-        filter_power(bank_ref, formed.at[n], out_refs[n], tot_parts.at[n])
-    total = tot_parts[0]
-    for n in range(1, count):
-        total = total + tot_parts[n]
-    tot_ref[...] = total
+    for chunk in CHUNKS:
+        calibrate_rows(v_ref, g_ref, cal_ref, *chunk)
+    for copy in tables:
+        copy.wait()
+
+
+def power_kernel(n, cal_ref, tab_ref, bank_ref, out_ref, tot_ref, formed):
+    for chunk in CHUNKS:
+        form(cal_ref, tab_ref.at[n], formed, *chunk)
+    filter_power(bank_ref, formed, out_ref, tot_ref)
 
 
 BRIEF = pl.CostEstimate(flops=100_000_000, bytes_accessed=10_000, transcendentals=0)
 POWER = jax.ShapeDtypeStruct((UP * FR, QUARTER), jnp.bfloat16)
 TOTAL = jax.ShapeDtypeStruct((UP, 128), jnp.float32)
-def calibrate(voltages, gains):
+def calibrate(order, voltages, gains, tables):
     flat = voltages.reshape(TS, 2, TILES, 128).transpose(0, 2, 1, 3).reshape(TS * KINDS, 128)
     return pl.pallas_call(
         calibrate_kernel,
-        in_specs=[VMEM, VMEM],
-        out_specs=VMEM,
-        out_shape=jax.ShapeDtypeStruct((TS, 2 * FEEDS), jnp.bfloat16),
-        compiler_params=PARAMS,
+        in_specs=[SMEM, VMEM, VMEM, HBM],
+        out_specs=[VMEM, VMEM],
+        out_shape=[
+            jax.ShapeDtypeStruct((TS, 2 * FEEDS), jnp.bfloat16),
+            jax.ShapeDtypeStruct((POL, 2 * FEEDS, 2 * QUARTER), jnp.bfloat16),
+        ],
+        scratch_shapes=[pltpu.SemaphoreType.DMA((POL,))],
+        compiler_params=pltpu.CompilerParams(vmem_limit_bytes=44 * 1024 * 1024),
         name="calibrate",
-    )(flat, gains)
-
-
-def quarter_powers(indices, calibrated, tables, bank):
-    count = len(indices)
+    )(order, flat, gains, tables)
+
+
+def quarter_power(n, calibrated, tables, bank):
     return pl.pallas_call(
-        functools.partial(power_kernel, count),
-        in_specs=[SMEM, VMEM, HBM, VMEM],
-        out_specs=[VMEM] * (count + 1),
-        out_shape=[POWER] * count + [TOTAL],
-        scratch_shapes=[
-            pltpu.VMEM((count, 2 * FEEDS, 2 * QUARTER), jnp.bfloat16),
-            pltpu.VMEM((count, TS, 2 * QUARTER), jnp.bfloat16),
-            pltpu.VMEM((count, UP, 128), jnp.float32),
-            pltpu.SemaphoreType.DMA((count,)),
-        ],
-        compiler_params=WHOLE,
+        functools.partial(power_kernel, n),
+        in_specs=[VMEM, VMEM, VMEM],
+        out_specs=[VMEM, VMEM],
+        out_shape=[POWER, TOTAL],
+        scratch_shapes=[pltpu.VMEM((TS, 2 * QUARTER), jnp.bfloat16)],
+        compiler_params=pltpu.CompilerParams(vmem_limit_bytes=32 * 1024 * 1024),
         cost_estimate=BRIEF,
-        name="quarter_powers",
-    )(jnp.stack(indices), calibrated, tables, bank)
+        name="quarter_power",
+    )(calibrated, tables, bank)
 
 
 def normalize_kernel(tot_ref, a_ref, b_ref, c_ref, d_ref, out_ref, inverse):
@@ -336,19 +328,19 @@
     core = lax.axis_index("freq") % CORES
     tables = jnp.asarray(beam_tables())
     bank = jnp.asarray(bank_matrix())
-    index = [(me + ahead) % POL for ahead in range(POL)]
+    order = (2, 1, 3, 0)
 
     def send(power, ahead):
         return lax.ppermute(power, "pol", [(i, (i + ahead) % POL) for i in range(POL)])
 
-    calibrated = calibrate(voltages[0, 0], gains[0, 0])
+    whose = (me + jnp.array(order, jnp.int32)) % POL
+    calibrated, tables = calibrate(whose, voltages[0, 0], gains[0, 0], tables)
     parts, totals = [], 0.0
-    for ahead in (2, 1, 3):
-        power, total = quarter_powers([index[ahead]], calibrated, tables, bank)
-        parts.append(send(power, ahead))
+    for n, ahead in enumerate(order):
+        power, total = quarter_power(n, calibrated, tables, bank)
+        parts.append(send(power, ahead) if ahead else power)
         totals = totals + total
-    own, total = quarter_powers([index[0]], calibrated, tables, bank)
-    normed = normalize(lax.psum(totals + total, "pol"), parts + [own])
+    normed = normalize(lax.psum(totals, "pol"), parts)
     alike = [[CORES * chip + c for chip in range(CHIPS)] for c in range(CORES)]
     turned = lax.all_to_all(
         normed.reshape(CHIPS, CORES, PAIR * UP * FR), "freq", 0, 0, tiled=True, axis_index_groups=alike

time: 102 us -> 98.4 us (0.965)
  Pallas kernels: 25 us -> 19.2 us
  blocking collectives: 23.6 us -> 26.3 us
    pallas_call x5, Pallas kernels: 20.1 us -> 15.7 us  [the longest x4 13 us: quarter_power(): pl.pallas_call(functools.partial(power_kernel, n), in_specs=[VMEM, VMEM,...]
    psum x1, blocking collectives: 9.36 us -> 11.7 us  [on_device(): normed = normalize(lax.psum(totals, 'pol'), parts)]
    pallas_call x1, Pallas kernels: 1.96 us -> 0.55 us  [normalize(): pl.pallas_call(normalize_kernel, in_specs=[VMEM] * (1 + POL), out_specs=V...]
    unnamed x18 -> x14, local copies, waits for them, and re-layouts: 4.38 us -> 3.47 us
  transfers between devices with their start and end apart: 4 -> 4, of which waited for: 1 -> 1; matrix products, arithmetic and copies ran while one was open for 1% -> 1% of each run, Pallas kernels for 13% -> 10%
where the time goes in v5:
time: 98.4 us; the launch traced here: 98 us
  starting transfers between devices  30.2 us (31%)
  blocking collectives  26.3 us (27%)
  Pallas kernels  19.2 us (20%)
  waiting for transfers between devices  14 us (14%)
  local copies, waits for them, and re-layouts  5.24 us (5%)
  other arithmetic  2.18 us (2%)
    all_to_all x1, starting transfers between devices, on_device(): lax.all_to_all(normed.reshape(CHIPS, CORES, PAIR * UP * FR), 'freq', 0, 0...  18.2 us
    all_to_all x1, blocking collectives, on_device(): lax.all_to_all(out, ('freq', 'pol'), 0, 0, tiled=True, axis_index_groups=...  14.5 us
    all_to_all x1, waiting for transfers between devices, on_device(): lax.all_to_all(normed.reshape(CHIPS, CORES, PAIR * UP * FR), 'freq', 0, 0...  14 us
    pallas_call x4, Pallas kernels, quarter_power(): pl.pallas_call(functools.partial(power_kernel, n), in_specs=[VMEM, VMEM,...  13 us
    ppermute x3, starting transfers between devices, send(): lax.ppermute(power, 'pol', [(i, (i + ahead) % POL) for i in range(POL)])  11.9 us
    psum x1, blocking collectives, on_device(): normed = normalize(lax.psum(totals, 'pol'), parts)  11.7 us
    unnamed x14, local copies, waits for them, and re-layouts  3.47 us
    pallas_call x1, Pallas kernels, dedisperse(): pl.pallas_call(dedisperse_kernel, in_specs=[SMEM, VMEM, VMEM, VMEM, VMEM]...  2.93 us
  transfers between devices with their start and end apart: 4, of which 1 were waited for; matrix products, arithmetic and copies ran while one was open for 1% of the time, Pallas kernels for 10%

profile of v5, /device:TPU:1, one launch (start us, length us, event | category | flops | bytes accessed | tf_op | source)
XLA Modules:
  0.0 98.0 jit_solution(2992478627841204289)
XLA Ops:
  0.0 0.0 copy-start
  0.0 0.7 and_select_fusion.1.q_ref
  0.7 0.0 copy-start.1
  0.7 1.8 %copy-done.1 = bf16[1,1,1392,2,512]{4,3,2,1,0:T(2,128)(2,1)S(1)} copy-done((bf16[1,1,1392,2,512]{4,3,2,1,0:T(2,128)(2,1)S(1)}, bf16[1,1,1392,2,512]{4,3,2,1,0:T(2,128)(2,1)}, u32[]{:S(2)}) %copy-start.1) | copy-done | bytes 2850840
  2.5 0.0 copy-start.4
  2.5 0.7 copy-done.4
  3.2 2.8 %calibrate.1 = (bf16[1392,1024]{1,0:T(8,128)(2,1)S(1)}, bf16[4,1024,512]{2,1,0:T(8,128)(2,1)S(1)}) custom-call(s32[4]{0:T(128)S(1)} %and_select_fusion.1.q_ref, bf16[11136,128]{1,0:T(8,128)(2,1)S(1)} %bitcast.14, f32[2,512]{1,0:T(2,128)S(1)} %bitcast.16, bf16[4,1024,512]{2,1,0:T(8,128)(2,1)} %constant.63.clone.tab_hbm), custom_call_target="tpu_custom_call" | custom-call | tf_op jit(solution)/shard_map/calibrate/pallas_call | solution.py:190
  6.0 0.0 copy-done
  6.0 3.4 %quarter_power.4 = (bf16[1152,256]{1,0:T(8,128)(2,1)}, f32[16,128]{1,0:T(8,128)S(1)}) custom-call(bf16[1392,1024]{1,0:T(8,128)(2,1)S(1)} %get-tuple-element.15.cal_ref, bf16[4,1024,512]{2,1,0:T(8,128)(2,1)S(1)} %get-tuple-element.16.tab_ref, bf16[256,736]{1,0:T(8,128)(2,1)S(1)} %copy-done), custom_call_target="tpu_custom_call" | custom-call | flops 100000000 | bytes 10000 | tf_op jit(solution)/shard_map/quarter_power/pallas_call | solution.py:205
  9.4 5.5 %collective-permute-start = (bf16[1152,256]{1,0:T(8,128)(2,1)}, bf16[1152,256]{1,0:T(8,128)(2,1)S(1)}, u32[]{:S(2)}, u32[]{:S(2)}) collective-permute-start(bf16[1152,256]{1,0:T(8,128)(2,1)} %get-tuple-element.21), channel_id=1, source_target_pairs={{0,2},{1,3},{2,0},{3,1},{4,6},{5,7},{6,4},{7,5},{8,10},{9,11},{10,... | collective-permute-start | bytes 1769480 | tf_op jit(solution)/shard_map/ppermute | solution.py:334
  14.9 3.4 %quarter_power.5 = (bf16[1152,256]{1,0:T(8,128)(2,1)}, f32[16,128]{1,0:T(8,128)S(1)}) custom-call(bf16[1392,1024]{1,0:T(8,128)(2,1)S(1)} %get-tuple-element.15.cal_ref, bf16[4,1024,512]{2,1,0:T(8,128)(2,1)S(1)} %get-tuple-element.16.tab_ref, bf16[256,736]{1,0:T(8,128)(2,1)S(1)} %copy-done), custom_call_target="tpu_custom_call" | custom-call | flops 100000000 | bytes 10000 | tf_op jit(solution)/shard_map/quarter_power/pallas_call | solution.py:205
  18.3 2.2 %collective-permute-start.1 = (bf16[1152,256]{1,0:T(8,128)(2,1)}, bf16[1152,256]{1,0:T(8,128)(2,1)S(1)}, u32[]{:S(2)}, u32[]{:S(2)}) collective-permute-start(bf16[1152,256]{1,0:T(8,128)(2,1)} %get-tuple-element.22), channel_id=1, source_target_pairs={{0,1},{1,2},{2,3},{3,0},{4,5},{5,6},{6,7},{7,4},{8,9},{9,10},{10,1... | collective-permute-start | bytes 1769480 | tf_op jit(solution)/shard_map/ppermute | solution.py:334
  20.5 3.4 %quarter_power.6 = (bf16[1152,256]{1,0:T(8,128)(2,1)}, f32[16,128]{1,0:T(8,128)S(1)}) custom-call(bf16[1392,1024]{1,0:T(8,128)(2,1)S(1)} %get-tuple-element.15.cal_ref, bf16[4,1024,512]{2,1,0:T(8,128)(2,1)S(1)} %get-tuple-element.16.tab_ref, bf16[256,736]{1,0:T(8,128)(2,1)S(1)} %copy-done), custom_call_target="tpu_custom_call" | custom-call | flops 100000000 | bytes 10000 | tf_op jit(solution)/shard_map/quarter_power/pallas_call | solution.py:205
  23.9 4.3 %collective-permute-start.2 = (bf16[1152,256]{1,0:T(8,128)(2,1)}, bf16[1152,256]{1,0:T(8,128)(2,1)S(1)}, u32[]{:S(2)}, u32[]{:S(2)}) collective-permute-start(bf16[1152,256]{1,0:T(8,128)(2,1)} %get-tuple-element.23), channel_id=1, source_target_pairs={{0,3},{1,0},{2,1},{3,2},{4,7},{5,4},{6,5},{7,6},{8,11},{9,8},{10,9... | collective-permute-start | bytes 1769480 | tf_op jit(solution)/shard_map/ppermute | solution.py:334
  28.2 2.7 %quarter_power.7 = (bf16[1152,256]{1,0:T(8,128)(2,1)S(1)}, f32[16,128]{1,0:T(8,128)S(1)}) custom-call(bf16[1392,1024]{1,0:T(8,128)(2,1)S(1)} %get-tuple-element.15.cal_ref, bf16[4,1024,512]{2,1,0:T(8,128)(2,1)S(1)} %get-tuple-element.16.tab_ref, bf16[256,736]{1,0:T(8,128)(2,1)S(1)} %copy-done), custom_call_target="tpu_custom_call" | custom-call | flops 100000000 | bytes 10000 | tf_op jit(solution)/shard_map/quarter_power/pallas_call | solution.py:205
  30.9 0.0 copy-start.5
  31.0 0.0 copy-start.6
  31.0 0.0 copy-start.2
  31.0 11.7 %psum.7.tot_ref = f32[16,128]{1,0:T(8,128)S(1)} all-reduce(f32[16,128]{1,0:T(8,128)S(1)} %add_add_fusion), channel_id=1, replica_groups=mesh['freq'=128,'pol'=4] {'pol'}, use_global_device_ids=true, to_apply=%region_1.2 | all-reduce | flops 2048 | bytes 16384 | tf_op jit(solution)/shard_map/psum | solution.py:343
  42.7 0.0 collective-permute-done.a_ref
  42.7 0.0 collective-permute-done.1.b_ref
  42.7 0.0 collective-permute-done.2.c_ref
  42.7 0.5 normalize.1
  43.3 1.0 %reshape.77 = bf16[64,2,2304]{2,1,0:T(2,128)(2,1)} reshape(bf16[128,2304]{1,0:T(8,128)(2,1)S(1)} %normalize.1) | data formatting | bytes 1179648 | tf_op jit(solution)/shard_map/reshape | solution.py:346
  44.3 18.2 %all-to-all-start = ((bf16[64,2,2304]{2,1,0:T(2,128)(2,1)}), bf16[64,2,2304]{2,1,0:T(2,128)(2,1)S(1)}, u32[]{:S(2)}, u32[]{:S(2)}) async-start(bf16[64,2,2304]{2,1,0:T(2,128)(2,1)} %reshape.77), calls=%async_computation | async-start | bytes 1179648 | tf_op jit(solution)/shard_map/all_to_all | solution.py:345
  62.6 0.0 copy-done.5
  62.6 0.0 copy-done.6
  62.6 0.6 compare_select_fusion
  63.9 0.1 reshape.79
  64.1 0.1 copy.17
  64.2 0.1 reshape.80
  64.3 0.1 copy.18
  64.4 0.1 copy.19
  64.5 0.1 iota_compare_fusion
  64.6 0.1 and_convert_fusion
  64.7 14.0 %all-to-all-done = bf16[64,2,2304]{2,1,0:T(2,128)(2,1)S(1)} async-done(((bf16[64,2,2304]{2,1,0:T(2,128)(2,1)}), bf16[64,2,2304]{2,1,0:T(2,128)(2,1)S(1)}, u32[]{:S(2)}, u32[]{:S(2)}) %all-to-all-start) | async-done | bytes 589856 | tf_op jit(solution)/shard_map/all_to_all | solution.py:345
  78.7 0.2 reshape.78.x_ref
  78.9 0.0 copy-done.2
  78.9 0.0 copy-start.3
  78.9 1.0 copy-done.3
  79.9 2.9 %dedisperse.1 = f32[8,2,24,128]{3,2,1,0:T(8,128)S(1)} custom-call(f32[1,1]{1,0:T(1,128)} %bitcast.scale_ref, bf16[128,2304]{1,0:T(8,128)(2,1)S(1)} %reshape.78.x_ref, bf16[896,256]{1,0:T(8,128)(2,1)S(1)} %bitcast.15, bf16[1152,128]{1,0:T(8,128)(2,1)S(1)} %copy-done.3, bf16[128,1736]{1,0:T(8,128)(2,1)S(1)} %copy-done.2), custom_call_target="tpu_custom_call" | custom-call | tf_op jit(solution)/shard_map/dedisperse/pallas_call | solution.py:301
  82.8 14.5 %all_to_all.10 = f32[8,2,24,128]{3,2,1,0:T(8,128)S(1)} all-to-all(f32[8,2,24,128]{3,2,1,0:T(8,128)S(1)} %dedisperse.1), channel_id=1, replica_groups={{0,1,2,3,4,5,6,7},{8,9,10,11,12,13,14,15},{16,17,18,19,20,21,22,23},{24..., dimensions={0} | all-to-all | bytes 393216 | tf_op jit(solution)/shard_map/all_to_all | solution.py:353
  97.3 0.7 slice_add_fusion
  (5 shorter events, 0.1 us)
Async XLA Ops:
  0.0 6.0 %copy-start = (bf16[256,736]{1,0:T(8,128)(2,1)S(1)}, bf16[256,736]{1,0:T(8,128)(2,1)}, u32[]{:S(2)}) copy-start(bf16[256,736]{1,0:T(8,128)(2,1)} %constant.64.clone.bank_ref) | copy-start | bytes 1130500
  0.7 1.8 %copy-start.1 = (bf16[1,1,1392,2,512]{4,3,2,1,0:T(2,128)(2,1)S(1)}, bf16[1,1,1392,2,512]{4,3,2,1,0:T(2,128)(2,1)}, u32[]{:S(2)}) copy-start(bf16[1,1,1392,2,512]{4,3,2,1,0:T(2,128)(2,1)} %param.9) | copy-start | bytes 8552452
  2.5 0.7 copy-start.4
  9.4 33.3 %collective-permute-start = (bf16[1152,256]{1,0:T(8,128)(2,1)}, bf16[1152,256]{1,0:T(8,128)(2,1)S(1)}, u32[]{:S(2)}, u32[]{:S(2)}) collective-permute-start(bf16[1152,256]{1,0:T(8,128)(2,1)} %get-tuple-element.21), channel_id=1, source_target_pairs={{0,2},{1,3},{2,0},{3,1},{4,6},{5,7},{6,4},{7,5},{8,10},{9,11},{10,... | collective-permute-start | bytes 1769480 | tf_op jit(solution)/shard_map/ppermute | solution.py:334
  18.3 24.4 %collective-permute-start.1 = (bf16[1152,256]{1,0:T(8,128)(2,1)}, bf16[1152,256]{1,0:T(8,128)(2,1)S(1)}, u32[]{:S(2)}, u32[]{:S(2)}) collective-permute-start(bf16[1152,256]{1,0:T(8,128)(2,1)} %get-tuple-element.22), channel_id=1, source_target_pairs={{0,1},{1,2},{2,3},{3,0},{4,5},{5,6},{6,7},{7,4},{8,9},{9,10},{10,1... | collective-permute-start | bytes 1769480 | tf_op jit(solution)/shard_map/ppermute | solution.py:334
  23.9 18.8 %collective-permute-start.2 = (bf16[1152,256]{1,0:T(8,128)(2,1)}, bf16[1152,256]{1,0:T(8,128)(2,1)S(1)}, u32[]{:S(2)}, u32[]{:S(2)}) collective-permute-start(bf16[1152,256]{1,0:T(8,128)(2,1)} %get-tuple-element.23), channel_id=1, source_target_pairs={{0,3},{1,0},{2,1},{3,2},{4,7},{5,4},{6,5},{7,6},{8,11},{9,8},{10,9... | collective-permute-start | bytes 1769480 | tf_op jit(solution)/shard_map/ppermute | solution.py:334
  30.9 31.7 %copy-start.5 = (s32[2048]{0:T(1024)S(1)}, s32[2048]{0:T(1024)}, u32[]{:S(2)}) copy-start(s32[2048]{0:T(1024)} %param.11) | copy-start | bytes 24580
  31.0 31.7 %copy-start.6 = (s32[2048]{0:T(1024)S(1)}, s32[2048]{0:T(1024)}, u32[]{:S(2)}) copy-start(s32[2048]{0:T(1024)} %param.12) | copy-start | bytes 24580
  31.0 47.9 %copy-start.2 = (bf16[128,1736]{1,0:T(8,128)(2,1)S(1)}, bf16[128,1736]{1,0:T(8,128)(2,1)}, u32[]{:S(2)}) copy-start(bf16[128,1736]{1,0:T(8,128)(2,1)} %constant.67.clone.trial_ref) | copy-start | bytes 1333252
  44.3 34.3 %all-to-all-start = ((bf16[64,2,2304]{2,1,0:T(2,128)(2,1)}), bf16[64,2,2304]{2,1,0:T(2,128)(2,1)S(1)}, u32[]{:S(2)}, u32[]{:S(2)}) async-start(bf16[64,2,2304]{2,1,0:T(2,128)(2,1)} %reshape.77), calls=%async_computation | async-start | bytes 1179648 | tf_op jit(solution)/shard_map/all_to_all | solution.py:345
  78.9 1.0 copy-start.3

commit v6 on v5

--- a/solution.py
+++ b/solution.py
@@ -164,9 +164,13 @@
         tot_ref[u : u + 1, :] = jnp.broadcast_to(jnp.sum(part, keepdims=True), (1, 128))
 
 
+ORDER = (2, 1, 3, 0)
+
+
 def calibrate_kernel(q_ref, v_ref, g_ref, tab_hbm, cal_ref, tab_ref, tab_sems):
     tables = [
-        pltpu.make_async_copy(tab_hbm.at[q_ref[n]], tab_ref.at[n], tab_sems.at[n]) for n in range(POL)
+        pltpu.make_async_copy(tab_hbm.at[(q_ref[0] + ahead) % POL], tab_ref.at[n], tab_sems.at[n])
+        for n, ahead in enumerate(ORDER)
     ]
     for copy in tables:
         copy.start()
@@ -215,8 +219,9 @@
 
 
 def normalize_kernel(tot_ref, a_ref, b_ref, c_ref, d_ref, out_ref, inverse):
+    means = (tot_ref[0] + tot_ref[1] + tot_ref[2] + tot_ref[3]) * (1.0 / (BEAMS * FR))
     for u in range(UP):
-        mean = tot_ref[u : u + 1, :] * (1.0 / (BEAMS * FR))
+        mean = means[u : u + 1, :]
         inverse[u * MG : (u + 1) * MG, :] = jnp.broadcast_to(1.0 / (mean + EPSILON), (MG, 128))
     scale = inverse[...]
     for g in range(BLOCKS):
@@ -328,19 +333,16 @@
     core = lax.axis_index("freq") % CORES
     tables = jnp.asarray(beam_tables())
     bank = jnp.asarray(bank_matrix())
-    order = (2, 1, 3, 0)
-
     def send(power, ahead):
         return lax.ppermute(power, "pol", [(i, (i + ahead) % POL) for i in range(POL)])
 
-    whose = (me + jnp.array(order, jnp.int32)) % POL
-    calibrated, tables = calibrate(whose, voltages[0, 0], gains[0, 0], tables)
+    calibrated, tables = calibrate(me.reshape(1), voltages[0, 0], gains[0, 0], tables)
     parts, totals = [], 0.0
-    for n, ahead in enumerate(order):
+    for n, ahead in enumerate(ORDER):
         power, total = quarter_power(n, calibrated, tables, bank)
         parts.append(send(power, ahead) if ahead else power)
         totals = totals + total
-    normed = normalize(lax.psum(totals, "pol"), parts)
+    normed = normalize(lax.all_to_all(jnp.broadcast_to(totals, (POL, UP, 128)), "pol", 0, 0, tiled=True), parts)
     alike = [[CORES * chip + c for chip in range(CHIPS)] for c in range(CORES)]
     turned = lax.all_to_all(
         normed.reshape(CHIPS, CORES, PAIR * UP * FR), "freq", 0, 0, tiled=True, axis_index_groups=alike

time: 98.4 us -> 93.9 us (0.954)
  Pallas kernels: 19.2 us -> 16.6 us
  waiting for transfers between devices: 14 us -> 16 us
  blocking collectives: 26.3 us -> 24.5 us
    psum x1 -> x0, blocking collectives: 11.7 us -> none  [on_device(): normed = normalize(lax.psum(totals, 'pol'), parts)]
    all_to_all x0 -> x1, blocking collectives: none -> 10.7 us  [on_device(): lax.all_to_all(jnp.broadcast_to(totals, (POL, UP, 128)), 'pol', 0, 0, til...]
    pallas_call x4, Pallas kernels: 13 us -> 10.9 us  [quarter_power(): pl.pallas_call(functools.partial(power_kernel, n), in_specs=[VMEM, VMEM,...]
    all_to_all x1, waiting for transfers between devices: 14 us -> 16 us  [on_device(): lax.all_to_all(normed.reshape(CHIPS, CORES, PAIR * UP * FR), 'freq', 0, 0...]
  transfers between devices with their start and end apart: 4 -> 4, of which waited for: 1 -> 1; matrix products, arithmetic and copies ran while one was open for 1% -> 1% of each run, Pallas kernels for 10% -> 9%
where the time goes in v6:
time: 93.9 us; the launch traced here: 93.5 us
  starting transfers between devices  29.7 us (32%)
  blocking collectives  24.5 us (26%)
  Pallas kernels  16.6 us (18%)
  waiting for transfers between devices  16 us (17%)
  local copies, waits for them, and re-layouts  4.34 us (5%)
  other arithmetic  1.47 us (2%)
  between operations  0.94 us (1%)
    all_to_all x1, starting transfers between devices, on_device(): lax.all_to_all(normed.reshape(CHIPS, CORES, PAIR * UP * FR), 'freq', 0, 0...  17.7 us
    all_to_all x1, waiting for transfers between devices, on_device(): lax.all_to_all(normed.reshape(CHIPS, CORES, PAIR * UP * FR), 'freq', 0, 0...  16 us
    all_to_all x1, blocking collectives, on_device(): lax.all_to_all(out, ('freq', 'pol'), 0, 0, tiled=True, axis_index_groups=...  13.7 us
    ppermute x3, starting transfers between devices, send(): lax.ppermute(power, 'pol', [(i, (i + ahead) % POL) for i in range(POL)])  12 us
    pallas_call x4, Pallas kernels, quarter_power(): pl.pallas_call(functools.partial(power_kernel, n), in_specs=[VMEM, VMEM,...  10.9 us
    all_to_all x1, blocking collectives, on_device(): lax.all_to_all(jnp.broadcast_to(totals, (POL, UP, 128)), 'pol', 0, 0, til...  10.7 us
    pallas_call x1, Pallas kernels, dedisperse(): pl.pallas_call(dedisperse_kernel, in_specs=[SMEM, VMEM, VMEM, VMEM, VMEM]...  2.93 us
    unnamed x14, local copies, waits for them, and re-layouts  2.57 us
  transfers between devices with their start and end apart: 4, of which 1 were waited for; matrix products, arithmetic and copies ran while one was open for 1% of the time, Pallas kernels for 9%

profile of v6, /device:TPU:1, one launch (start us, length us, event | category | flops | bytes accessed | tf_op | source)
XLA Modules:
  0.0 93.5 jit_solution(1496478140090660851)
XLA Ops:
  0.0 0.0 copy-start
  0.0 0.0 copy-start.1
  0.0 1.9 %copy-done.1 = bf16[1,1,1392,2,512]{4,3,2,1,0:T(2,128)(2,1)S(1)} copy-done((bf16[1,1,1392,2,512]{4,3,2,1,0:T(2,128)(2,1)S(1)}, bf16[1,1,1392,2,512]{4,3,2,1,0:T(2,128)(2,1)}, u32[]{:S(2)}) %copy-start.1) | copy-done | bytes 2850840
  1.9 0.0 copy-start.4
  1.9 0.7 copy-done.4
  2.5 2.2 %calibrate.1 = (bf16[1392,1024]{1,0:T(8,128)(2,1)S(1)}, bf16[4,1024,512]{2,1,0:T(8,128)(2,1)S(1)}) custom-call(s32[1]{0:T(128)} %bitcast.1.q_ref, bf16[11136,128]{1,0:T(8,128)(2,1)S(1)} %bitcast.15, f32[2,512]{1,0:T(2,128)S(1)} %bitcast.17, bf16[4,1024,512]{2,1,0:T(8,128)(2,1)} %constant.47.clone.tab_hbm), custom_call_target="tpu_custom_call" | custom-call | tf_op jit(solution)/shard_map/calibrate/pallas_call | solution.py:194
  4.8 0.0 copy-done
  4.8 2.7 %quarter_power.4 = (bf16[1152,256]{1,0:T(8,128)(2,1)S(1)}, f32[16,128]{1,0:T(8,128)S(1)}) custom-call(bf16[1392,1024]{1,0:T(8,128)(2,1)S(1)} %get-tuple-element.15.cal_ref, bf16[4,1024,512]{2,1,0:T(8,128)(2,1)S(1)} %get-tuple-element.16.tab_ref, bf16[256,736]{1,0:T(8,128)(2,1)S(1)} %copy-done), custom_call_target="tpu_custom_call" | custom-call | flops 100000000 | bytes 10000 | tf_op jit(solution)/shard_map/quarter_power/pallas_call | solution.py:209
  7.5 5.5 %collective-permute-start = (bf16[1152,256]{1,0:T(8,128)(2,1)S(1)}, bf16[1152,256]{1,0:T(8,128)(2,1)S(1)}, u32[]{:S(2)}, u32[]{:S(2)}) collective-permute-start(bf16[1152,256]{1,0:T(8,128)(2,1)S(1)} %get-tuple-element.21), channel_id=1, source_target_pairs={{0,2},{1,3},{2,0},{3,1},{4,6},{5,7},{6,4},{7,5},{8,10},{9,11},{10,... | collective-permute-start | bytes 1769480 | tf_op jit(solution)/shard_map/ppermute | solution.py:337
  13.0 2.7 %quarter_power.5 = (bf16[1152,256]{1,0:T(8,128)(2,1)S(1)}, f32[16,128]{1,0:T(8,128)S(1)}) custom-call(bf16[1392,1024]{1,0:T(8,128)(2,1)S(1)} %get-tuple-element.15.cal_ref, bf16[4,1024,512]{2,1,0:T(8,128)(2,1)S(1)} %get-tuple-element.16.tab_ref, bf16[256,736]{1,0:T(8,128)(2,1)S(1)} %copy-done), custom_call_target="tpu_custom_call" | custom-call | flops 100000000 | bytes 10000 | tf_op jit(solution)/shard_map/quarter_power/pallas_call | solution.py:209
  15.8 2.2 %collective-permute-start.1 = (bf16[1152,256]{1,0:T(8,128)(2,1)S(1)}, bf16[1152,256]{1,0:T(8,128)(2,1)S(1)}, u32[]{:S(2)}, u32[]{:S(2)}) collective-permute-start(bf16[1152,256]{1,0:T(8,128)(2,1)S(1)} %get-tuple-element.22), channel_id=1, source_target_pairs={{0,1},{1,2},{2,3},{3,0},{4,5},{5,6},{6,7},{7,4},{8,9},{9,10},{10,1... | collective-permute-start | bytes 1769480 | tf_op jit(solution)/shard_map/ppermute | solution.py:337
  18.0 2.7 %quarter_power.6 = (bf16[1152,256]{1,0:T(8,128)(2,1)S(1)}, f32[16,128]{1,0:T(8,128)S(1)}) custom-call(bf16[1392,1024]{1,0:T(8,128)(2,1)S(1)} %get-tuple-element.15.cal_ref, bf16[4,1024,512]{2,1,0:T(8,128)(2,1)S(1)} %get-tuple-element.16.tab_ref, bf16[256,736]{1,0:T(8,128)(2,1)S(1)} %copy-done), custom_call_target="tpu_custom_call" | custom-call | flops 100000000 | bytes 10000 | tf_op jit(solution)/shard_map/quarter_power/pallas_call | solution.py:209
  20.7 4.3 %collective-permute-start.2 = (bf16[1152,256]{1,0:T(8,128)(2,1)S(1)}, bf16[1152,256]{1,0:T(8,128)(2,1)S(1)}, u32[]{:S(2)}, u32[]{:S(2)}) collective-permute-start(bf16[1152,256]{1,0:T(8,128)(2,1)S(1)} %get-tuple-element.23), channel_id=1, source_target_pairs={{0,3},{1,0},{2,1},{3,2},{4,7},{5,4},{6,5},{7,6},{8,11},{9,8},{10,9... | collective-permute-start | bytes 1769480 | tf_op jit(solution)/shard_map/ppermute | solution.py:337
  25.0 2.7 %quarter_power.7 = (bf16[1152,256]{1,0:T(8,128)(2,1)S(1)}, f32[16,128]{1,0:T(8,128)S(1)}) custom-call(bf16[1392,1024]{1,0:T(8,128)(2,1)S(1)} %get-tuple-element.15.cal_ref, bf16[4,1024,512]{2,1,0:T(8,128)(2,1)S(1)} %get-tuple-element.16.tab_ref, bf16[256,736]{1,0:T(8,128)(2,1)S(1)} %copy-done), custom_call_target="tpu_custom_call" | custom-call | flops 100000000 | bytes 10000 | tf_op jit(solution)/shard_map/quarter_power/pallas_call | solution.py:209
  27.7 0.0 copy-start.5
  27.7 0.0 copy-start.6
  27.8 0.0 copy-start.2
  27.8 0.0 copy-start.3
  27.8 10.7 %all_to_all.15.tot_ref = f32[4,16,128]{2,1,0:T(8,128)S(1)} all-to-all(f32[4,16,128]{2,1,0:T(8,128)S(1)} %broadcast_in_dim.13), channel_id=1, replica_groups=mesh['freq'=128,'pol'=4] {'pol'}, dimensions={0} | all-to-all | bytes 65536 | tf_op jit(solution)/shard_map/all_to_all | solution.py:345
  38.6 0.0 collective-permute-done.a_ref
  38.6 0.0 collective-permute-done.1.b_ref
  38.6 0.0 collective-permute-done.2.c_ref
  38.6 0.5 normalize.1
  39.1 1.0 %reshape.81 = bf16[64,2,2304]{2,1,0:T(2,128)(2,1)} reshape(bf16[128,2304]{1,0:T(8,128)(2,1)S(1)} %normalize.1) | data formatting | bytes 1179648 | tf_op jit(solution)/shard_map/reshape | solution.py:348
  40.1 17.7 %all-to-all-start.1 = ((bf16[64,2,2304]{2,1,0:T(2,128)(2,1)}), bf16[64,2,2304]{2,1,0:T(2,128)(2,1)S(1)}, u32[]{:S(2)}, u32[]{:S(2)}) async-start(bf16[64,2,2304]{2,1,0:T(2,128)(2,1)} %reshape.81), calls=%async_computation.1 | async-start | bytes 1179648 | tf_op jit(solution)/shard_map/all_to_all | solution.py:347
  57.8 0.0 copy-done.5
  57.9 0.0 copy-done.6
  57.9 0.6 compare_select_fusion
  59.2 0.1 reshape.83
  59.4 0.1 copy.16
  59.4 0.1 reshape.84
  59.5 0.1 copy.17
  59.7 0.1 copy.18
  59.7 0.1 iota_compare_fusion
  59.8 0.1 and_convert_fusion
  59.9 16.0 %all-to-all-done.1 = bf16[64,2,2304]{2,1,0:T(2,128)(2,1)S(1)} async-done(((bf16[64,2,2304]{2,1,0:T(2,128)(2,1)}), bf16[64,2,2304]{2,1,0:T(2,128)(2,1)S(1)}, u32[]{:S(2)}, u32[]{:S(2)}) %all-to-all-start.1) | async-done | bytes 589856 | tf_op jit(solution)/shard_map/all_to_all | solution.py:347
  76.0 0.2 reshape.82.x_ref
  76.2 0.0 copy-done.2
  76.2 0.0 copy-done.3
  76.2 2.9 %dedisperse.1 = f32[8,2,24,128]{3,2,1,0:T(8,128)S(1)} custom-call(f32[1,1]{1,0:T(1,128)} %bitcast.scale_ref, bf16[128,2304]{1,0:T(8,128)(2,1)S(1)} %reshape.82.x_ref, bf16[896,256]{1,0:T(8,128)(2,1)S(1)} %bitcast.16, bf16[1152,128]{1,0:T(8,128)(2,1)S(1)} %copy-done.3, bf16[128,1736]{1,0:T(8,128)(2,1)S(1)} %copy-done.2), custom_call_target="tpu_custom_call" | custom-call | tf_op jit(solution)/shard_map/dedisperse/pallas_call | solution.py:306
  79.1 13.7 %all_to_all.16 = f32[8,2,24,128]{3,2,1,0:T(8,128)S(1)} all-to-all(f32[8,2,24,128]{3,2,1,0:T(8,128)S(1)} %dedisperse.1), channel_id=1, replica_groups={{0,1,2,3,4,5,6,7},{8,9,10,11,12,13,14,15},{16,17,18,19,20,21,22,23},{24..., dimensions={0} | all-to-all | bytes 393216 | tf_op jit(solution)/shard_map/all_to_all | solution.py:355
  92.9 0.7 slice_add_fusion
  (6 shorter events, 0.1 us)
Async XLA Ops:
  0.0 4.8 %copy-start = (bf16[256,736]{1,0:T(8,128)(2,1)S(1)}, bf16[256,736]{1,0:T(8,128)(2,1)}, u32[]{:S(2)}) copy-start(bf16[256,736]{1,0:T(8,128)(2,1)} %constant.48.clone.bank_ref) | copy-start | bytes 1130500
  0.0 1.9 %copy-start.1 = (bf16[1,1,1392,2,512]{4,3,2,1,0:T(2,128)(2,1)S(1)}, bf16[1,1,1392,2,512]{4,3,2,1,0:T(2,128)(2,1)}, u32[]{:S(2)}) copy-start(bf16[1,1,1392,2,512]{4,3,2,1,0:T(2,128)(2,1)} %param.8) | copy-start | bytes 8552452
  1.9 0.7 copy-start.4
  7.5 31.0 %collective-permute-start = (bf16[1152,256]{1,0:T(8,128)(2,1)S(1)}, bf16[1152,256]{1,0:T(8,128)(2,1)S(1)}, u32[]{:S(2)}, u32[]{:S(2)}) collective-permute-start(bf16[1152,256]{1,0:T(8,128)(2,1)S(1)} %get-tuple-element.21), channel_id=1, source_target_pairs={{0,2},{1,3},{2,0},{3,1},{4,6},{5,7},{6,4},{7,5},{8,10},{9,11},{10,... | collective-permute-start | bytes 1769480 | tf_op jit(solution)/shard_map/ppermute | solution.py:337
  15.8 22.8 %collective-permute-start.1 = (bf16[1152,256]{1,0:T(8,128)(2,1)S(1)}, bf16[1152,256]{1,0:T(8,128)(2,1)S(1)}, u32[]{:S(2)}, u32[]{:S(2)}) collective-permute-start(bf16[1152,256]{1,0:T(8,128)(2,1)S(1)} %get-tuple-element.22), channel_id=1, source_target_pairs={{0,1},{1,2},{2,3},{3,0},{4,5},{5,6},{6,7},{7,4},{8,9},{9,10},{10,1... | collective-permute-start | bytes 1769480 | tf_op jit(solution)/shard_map/ppermute | solution.py:337
  20.7 17.8 %collective-permute-start.2 = (bf16[1152,256]{1,0:T(8,128)(2,1)S(1)}, bf16[1152,256]{1,0:T(8,128)(2,1)S(1)}, u32[]{:S(2)}, u32[]{:S(2)}) collective-permute-start(bf16[1152,256]{1,0:T(8,128)(2,1)S(1)} %get-tuple-element.23), channel_id=1, source_target_pairs={{0,3},{1,0},{2,1},{3,2},{4,7},{5,4},{6,5},{7,6},{8,11},{9,8},{10,9... | collective-permute-start | bytes 1769480 | tf_op jit(solution)/shard_map/ppermute | solution.py:337
  27.7 30.1 %copy-start.5 = (s32[2048]{0:T(1024)S(1)}, s32[2048]{0:T(1024)}, u32[]{:S(2)}) copy-start(s32[2048]{0:T(1024)} %param.10) | copy-start | bytes 24580
  27.7 30.1 %copy-start.6 = (s32[2048]{0:T(1024)S(1)}, s32[2048]{0:T(1024)}, u32[]{:S(2)}) copy-start(s32[2048]{0:T(1024)} %param.11) | copy-start | bytes 24580
  27.8 48.4 %copy-start.2 = (bf16[128,1736]{1,0:T(8,128)(2,1)S(1)}, bf16[128,1736]{1,0:T(8,128)(2,1)}, u32[]{:S(2)}) copy-start(bf16[128,1736]{1,0:T(8,128)(2,1)} %constant.50.clone.trial_ref) | copy-start | bytes 1333252
  27.8 48.4 %copy-start.3 = (bf16[1152,128]{1,0:T(8,128)(2,1)S(1)}, bf16[1152,128]{1,0:T(8,128)(2,1)}, u32[]{:S(2)}) copy-start(bf16[1152,128]{1,0:T(8,128)(2,1)} %constant.49.clone.fold_ref) | copy-start | bytes 884740
  40.1 35.8 %all-to-all-start.1 = ((bf16[64,2,2304]{2,1,0:T(2,128)(2,1)}), bf16[64,2,2304]{2,1,0:T(2,128)(2,1)S(1)}, u32[]{:S(2)}, u32[]{:S(2)}) async-start(bf16[64,2,2304]{2,1,0:T(2,128)(2,1)} %reshape.81), calls=%async_computation.1 | async-start | bytes 1179648 | tf_op jit(solution)/shard_map/all_to_all | solution.py:347
